TPU v7x, 128 devices: a whole 4x4x4 slice. The times are simulated.
128 devices in a mesh: ctx: 64 (over z, y, x), tp: 2 (over core).
Axes of the slice: x: 4, y: 4, z: 4, core: 2. Of those that a mesh axis runs over, the one named last changes fastest.
Arguments:
- queries: bfloat16 [16384, 8192], P(('ctx', 'tp')), may hold values from -6 to 6
- key_matrix: bfloat16 [16384, 1024], P(('ctx', 'tp')), may hold values from -6 to 6
- value_matrix: bfloat16 [16384, 1024], P(('ctx', 'tp')), may hold values from -6 to 6
- attention_output: bfloat16 [16384, 8192], P(('ctx', 'tp')), may hold values from -6 to 6
- output_gradient: bfloat16 [16384, 8192], P(('ctx', 'tp')), may hold values from -6 to 6
- lengths: int32 [256], replicated, may hold values from 1 to 1792, 16384 in all
Outputs:
- query_grad: bfloat16 [16384, 8192], P(('ctx', 'tp'))
- key_gradient: bfloat16 [16384, 1024], P(('ctx', 'tp'))
- value_gradient: bfloat16 [16384, 1024], P(('ctx', 'tp'))
Inputs may be any that keep to these rules, and one draw needn't show every extreme that they name: The lengths sum to 16384; the longest document has exactly 1792 tokens.
All inputs are finite; a program needn't handle non-finite values.
Results may differ from a plain program's by a relative error of at most 0.005.
Values may be sent and summed in bfloat16 or wider, within the bound.
A program may use at most 128 MiB of HBM per device.

v0:
```python
import jax
import jax.numpy as jnp
from jax import lax
from jax.sharding import PartitionSpec as P

HEAD_SIZE = 128


NEG = -1e30


def from_behind(x, axis, by):
    peers = lax.axis_size(axis)
    pairs = [(i, i + by) for i in range(peers) if 0 <= i + by < peers]
    return lax.ppermute(x, axis, pairs)


def document_index(positions, lengths):
    starts = jnp.cumsum(lengths, dtype=jnp.int32) - lengths
    starts_hit = (starts[None, :] <= positions[:, None]).astype(jnp.int32)
    return jnp.sum(starts_hit, axis=1) - 1


def per_device(queries, key_matrix, value_matrix, attention_output, output_gradient, lengths):
    tp_count = lax.axis_size("tp")
    reach_count = max(1, lax.axis_size("ctx") // 8 - 1)
    seq_rows = queries.shape[0]
    heads_q = queries.shape[1] // HEAD_SIZE
    heads_kv = key_matrix.shape[1] // HEAD_SIZE
    q_loc, g_loc, o_loc, k_loc, v_loc = (
        lax.all_to_all(
            queries.reshape(seq_rows, heads_q, HEAD_SIZE),
            "tp",
            split_axis=1,
            concat_axis=0,
            tiled=True,
        ),
        lax.all_to_all(
            output_gradient.reshape(seq_rows, heads_q, HEAD_SIZE),
            "tp",
            split_axis=1,
            concat_axis=0,
            tiled=True,
        ),
        lax.all_to_all(
            attention_output.reshape(seq_rows, heads_q, HEAD_SIZE),
            "tp",
            split_axis=1,
            concat_axis=0,
            tiled=True,
        ),
        lax.all_to_all(
            key_matrix.reshape(seq_rows, heads_kv, HEAD_SIZE),
            "tp",
            split_axis=1,
            concat_axis=0,
            tiled=True,
        ),
        lax.all_to_all(
            value_matrix.reshape(seq_rows, heads_kv, HEAD_SIZE),
            "tp",
            split_axis=1,
            concat_axis=0,
            tiled=True,
        ),
    )
    shard_len = seq_rows * tp_count
    local_kv = heads_kv // tp_count
    query_group_width = heads_q // heads_kv
    q_loc = q_loc.reshape(shard_len, local_kv, query_group_width, HEAD_SIZE)
    g_loc = g_loc.reshape(shard_len, local_kv, query_group_width, HEAD_SIZE)
    o_loc = o_loc.reshape(shard_len, local_kv, query_group_width, HEAD_SIZE)
    inv_root = HEAD_SIZE ** (-0.5)
    first_pos = lax.axis_index("ctx") * shard_len
    q_pos = first_pos + jnp.arange(shard_len, dtype=jnp.int32)
    q_doc = document_index(q_pos, lengths)
    row_delta = jnp.einsum("ikgd,ikgd->kgi", g_loc, o_loc, preferred_element_type=jnp.float32)[
        ..., None
    ]
    kv_pair = jnp.stack([k_loc, v_loc], axis=0)[:, None]
    pieces = [kv_pair]
    for offset in range(1, reach_count + 1):
        pieces.append(from_behind(kv_pair, "ctx", offset))
    kv_stack = jnp.concatenate(pieces, axis=1)
    block_count = reach_count + 1
    key_total = block_count * shard_len
    keys_win = kv_stack[0].reshape(key_total, local_kv, HEAD_SIZE)
    values_win = kv_stack[1].reshape(key_total, local_kv, HEAD_SIZE)
    key_ids = jnp.arange(key_total, dtype=jnp.int32)
    key_pos = first_pos - key_ids // shard_len * shard_len + key_ids % shard_len
    key_doc = document_index(key_pos, lengths)
    key_block = min(512, key_total)
    step_count = key_total // key_block

    def block_view(block_index):
        block_start = block_index * key_block
        k_blk = lax.dynamic_slice_in_dim(keys_win, block_start, key_block, 0)
        v_blk = lax.dynamic_slice_in_dim(values_win, block_start, key_block, 0)
        pos_blk = lax.dynamic_slice_in_dim(key_pos, block_start, key_block, 0)
        doc_blk = lax.dynamic_slice_in_dim(key_doc, block_start, key_block, 0)
        allowed = (q_doc[:, None] == doc_blk[None, :]) & (pos_blk[None, :] <= q_pos[:, None])
        return (k_blk, v_blk, allowed)

    def stats_update(block_index, state):
        k_blk, v_blk, allowed = block_view(block_index)
        scores = (
            jnp.einsum("ikgd,jkd->kgij", q_loc, k_blk, preferred_element_type=jnp.float32)
            * inv_root
        )
        masked = jnp.where(allowed, scores, NEG)
        new_top = jnp.maximum(state[0], jnp.max(masked, axis=-1, keepdims=True))
        new_sum = state[1] * jnp.exp(state[0] - new_top) + jnp.sum(
            jnp.where(allowed, jnp.exp(masked - new_top), 0.0), axis=-1, keepdims=True
        )
        return (new_top, new_sum)

    stat_shape = (local_kv, query_group_width, shard_len, 1)
    row_top, row_total = lax.fori_loop(
        0,
        step_count,
        stats_update,
        (jnp.full(stat_shape, NEG, jnp.float32), jnp.zeros(stat_shape, jnp.float32)),
    )
    log_total = row_top + jnp.log(row_total)

    def grad_update(block_index, state):
        k_blk, v_blk, allowed = block_view(block_index)
        scores = (
            jnp.einsum("ikgd,jkd->kgij", q_loc, k_blk, preferred_element_type=jnp.float32)
            * inv_root
        )
        prob_full = jnp.where(allowed, jnp.exp(jnp.where(allowed, scores, NEG) - log_total), 0.0)
        probs_low = prob_full.astype(jnp.bfloat16)
        dprobs = jnp.einsum("ikgd,jkd->kgij", g_loc, v_blk, preferred_element_type=jnp.float32)
        ds_low = (prob_full * (dprobs - row_delta)).astype(jnp.bfloat16)
        dq_new = (
            state[0]
            + jnp.einsum("kgij,jkd->ikgd", ds_low, k_blk, preferred_element_type=jnp.float32)
            * inv_root
        )
        dk_blk = (
            jnp.einsum("kgij,ikgd->jkd", ds_low, q_loc, preferred_element_type=jnp.float32)
            * inv_root
        )
        dv_blk = jnp.einsum("kgij,ikgd->jkd", probs_low, g_loc, preferred_element_type=jnp.float32)
        block_start = block_index * key_block
        dk_all = lax.dynamic_update_slice_in_dim(state[1], dk_blk, block_start, 0)
        dv_all = lax.dynamic_update_slice_in_dim(state[2], dv_blk, block_start, 0)
        return (dq_new, dk_all, dv_all)

    zero_win = jnp.zeros((key_total, local_kv, HEAD_SIZE), jnp.float32)
    dq_acc, dk_win, dv_win = lax.fori_loop(
        0,
        step_count,
        grad_update,
        (
            jnp.zeros((shard_len, local_kv, query_group_width, HEAD_SIZE), jnp.float32),
            zero_win,
            zero_win,
        ),
    )
    partials = jnp.stack([dk_win, dv_win], axis=0).reshape(
        2, block_count, shard_len, local_kv, HEAD_SIZE
    )
    own_grads = partials[:, 0]
    for offset in range(1, reach_count + 1):
        own_grads = own_grads + from_behind(partials[:, offset], "ctx", -offset)
    q_out = dq_acc.astype(jnp.bfloat16).reshape(shard_len, local_kv * query_group_width, HEAD_SIZE)
    k_out = own_grads[0].astype(jnp.bfloat16)
    v_out = own_grads[1].astype(jnp.bfloat16)
    q_back, k_back, v_back = (
        lax.all_to_all(q_out, "tp", split_axis=0, concat_axis=1, tiled=True),
        lax.all_to_all(k_out, "tp", split_axis=0, concat_axis=1, tiled=True),
        lax.all_to_all(v_out, "tp", split_axis=0, concat_axis=1, tiled=True),
    )
    return (
        q_back.reshape(seq_rows, heads_q * HEAD_SIZE),
        k_back.reshape(seq_rows, heads_kv * HEAD_SIZE),
        v_back.reshape(seq_rows, heads_kv * HEAD_SIZE),
    )


def solution(mesh):
    in_specs = (
        P(("ctx", "tp"), None),
        P(("ctx", "tp"), None),
        P(("ctx", "tp"), None),
        P(("ctx", "tp"), None),
        P(("ctx", "tp"), None),
        P(),
    )
    out_specs = (P(("ctx", "tp"), None), P(("ctx", "tp"), None), P(("ctx", "tp"), None))
    return jax.shard_map(
        per_device, mesh=mesh, in_specs=in_specs, out_specs=out_specs, check_vma=False
    )
```

profile of v0, /device:TPU:65, one launch (start us, length us, event | category | flops | bytes accessed | tf_op | source)
XLA Modules:
  0.0 480.9 jit_solution(16461288231243723259)
XLA Ops:
  2.6 4.1 all-to-all-start
  8.7 3.5 all-to-all-start.1
  14.3 4.1 collective-permute-start.4
  18.4 3.2 collective-permute-start.3
  21.6 4.1 collective-permute-start.2
  25.7 3.4 collective-permute-start.1
  31.4 3.2 copy.179
  34.6 2.9 copy.180
  37.5 5.5 %all-to-all-start.4 = ((bf16[128,64,128]{2,0,1:T(8,128)(2,1)}), bf16[128,64,128]{2,0,1:T(8,128)(2,1)S(1)}, u32[]{:S(2)}, u32[]{:S(2)}) async-start(bf16[128,64,128]{2,0,1:T(8,128)(2,1)} %copy.180), calls=%async_computation.4 | async-start | bytes 4194304 | tf_op jit(solution)/shard_map/all_to_all | solution.py:45
  43.7 4.1 copy.169
  47.7 4.1 copy.170
  51.8 4.1 copy.175
  55.9 4.1 copy.176
  60.0 4.8 %all-to-all-start.3 = ((bf16[128,64,128]{2,0,1:T(8,128)(2,1)}), bf16[128,64,128]{2,0,1:T(8,128)(2,1)}, u32[]{:S(2)}, u32[]{:S(2)}) async-start(bf16[128,64,128]{2,0,1:T(8,128)(2,1)} %copy.176), calls=%async_computation.3 | async-start | bytes 4194304 | tf_op jit(solution)/shard_map/all_to_all | solution.py:38
  67.5 4.0 all-to-all-start.2
  71.6 3.1 copy.178
  81.0 3.9 copy.184
  84.9 5.5 %collective-permute-start.5 = (bf16[2,1,256,4,128]{4,2,3,0,1:T(8,128)(2,1)}, bf16[2,1,256,4,128]{4,2,3,0,1:T(8,128)(2,1)S(1)}, u32[]{:S(2)}, u32[]{:S(2)}) collective-permute-start(bf16[2,1,256,4,128]{4,2,3,0,1:T(8,128)(2,1)} %maximum_bitcast_fusion), channel_id=1, source_target_pairs={{0,12},{2,14},{4,16},{6,18},{8,20},{10,22},{12,24},{14,26},{16,28}... | collective-permute-start | bytes 1572872 | tf_op jit(solution)/shard_map/ppermute | solution.py:15
  91.6 5.1 %collective-permute-start.6 = (bf16[2,1,256,4,128]{4,2,3,0,1:T(8,128)(2,1)}, bf16[2,1,256,4,128]{4,2,3,0,1:T(8,128)(2,1)S(1)}, u32[]{:S(2)}, u32[]{:S(2)}) collective-permute-start(bf16[2,1,256,4,128]{4,2,3,0,1:T(8,128)(2,1)} %maximum_bitcast_fusion), channel_id=1, source_target_pairs={{0,14},{2,16},{4,18},{6,20},{8,22},{10,24},{12,26},{14,28},{16,30}... | collective-permute-start | bytes 1572872 | tf_op jit(solution)/shard_map/ppermute | solution.py:15
  101.2 4.1 collective-permute-done.5
  105.4 11.8 %collective-permute-done.6 = bf16[2,1,256,4,128]{4,2,3,0,1:T(8,128)(2,1)S(1)} collective-permute-done((bf16[2,1,256,4,128]{4,2,3,0,1:T(8,128)(2,1)}, bf16[2,1,256,4,128]{4,2,3,0,1:T(8,128)(2,1)S(1)}, u32[]{:S(2)}, u32[]{:S(2)}) %collective-permute-start.6) | collective-permute-done | bytes 524320 | tf_op jit(solution)/shard_map/ppermute | solution.py:15
  120.9 33.6 %while.34 = (s32[]{:T(128)}, f32[4,8,256,1]{2,1,0,3:T(8,128)S(1)}, f32[4,8,256,1]{2,1,0,3:T(8,128)S(1)}, s32[256]{0:T(256)S(1)}, s32[2048]{0:T(1024)S(1)}, /*ind...) while((s32[]{:T(128)}, f32[4,8,256,1]{2,1,0,3:T(8,128)S(1)}, ...), condition=%wide.region_7.8_spmd.clone, body=%wide.region_4.7_spmd.clone.sunk | while | flops 1107730688 | bytes 37010636 | solution.py:118
  121.2 3.7 fusion.99
  125.0 4.2 select_reduce_fusion.2
  129.6 3.7 fusion.99
  133.4 4.2 select_reduce_fusion.2
  138.0 3.7 fusion.99
  141.8 4.2 select_reduce_fusion.2
  146.5 3.7 fusion.99
  150.2 4.2 select_reduce_fusion.2
  159.0 136.2 %while.35 = (s32[]{:T(128)}, f32[256,4,8,128]{0,3,2,1:T(8,128)}, f32[2048,4,128]{2,0,1:T(8,128)}, f32[2048,4,128]{2,0,1:T(8,128)}, bf16[2048,4,128]{2,0,1:T(8,12...) while((s32[]{:T(128)}, f32[256,4,8,128]{0,3,2,1:T(8,128)}, ...), condition=%wide.region_9.10_spmd.clone, body=%wide.region_8.9_spmd.clone.sunk | while | flops 5422841856 | bytes 138394976 | solution.py:152
  159.4 9.3 %fusion.110 = f32[4,512,256,8]{2,1,3,0:T(8,128)} fusion(bf16[256,4,8,128]{3,0,2,1:T(8,128)(2,1)S(1)} %get-tuple-element.893, bf16[2048,4,128]{2,0,1:T(8,128)(2,1)} %get-tuple-element.889, s32[]{:T(128)S(6)} %select_n.137), kind=kOutput, calls=%fused_computation.31.clone.1 | convolution fusion | flops 1073741824 | bytes 19398660 | tf_op jit(solution)/shard_map/while/body/eval_jaxpr/ikgd,jkd->kgij/dot_general | solution.py:129
  168.7 8.7 %fusion.113 = f32[2048,4,128]{2,0,1:T(8,128)} fusion(f32[2048,4,128]{2,0,1:T(8,128)} %get-tuple-element.870, s32[]{:T(128)S(6)} %select_n.137, bf16[256,4,8,128]{3,0,2,1:T(8,128)(2,1)S(1)} %copy-done.6, f32[4,512,256,8]{2,1,3,0:T(8,128)} %fusion.110, f32[4,8,256]{2,1,0:T(8,128)S(1)} %bitcast.272, pred[256,512]{0,1:T(8,128)(4,1)S(1)} %compare_and_fusion.5), kind=kOutput, calls=%fused_computation.26.clone.1 | convolution fusion | flops 1094713344 | bytes 20086788 | tf_op jit(solution)/shard_map/while/body/eval_jaxpr/kgij,ikgd->jkd/dot_general | solution.py:145
  177.4 9.5 %fusion.111 = bf16[4,8,256,512]{2,3,1,0:T(8,128)(2,1)S(1)} fusion(f32[4,512,256,8]{2,1,3,0:T(8,128)} %fusion.110, bf16[256,4,8,128]{3,0,2,1:T(8,128)(2,1)} %get-tuple-element.896, f32[4,8,256]{2,1,0:T(8,128)S(1)} %bitcast.271, f32[4,8,256]{2,1,0:T(8,128)S(1)} %bitcast.273, pred[256,512]{0,1:T(8,128)(4,1)S(1)} %compare_and_fusion.5, ...), kind=kOutput, calls=%fused_computation.16.clone.1 | convolution fusion | flops 1103101952 | bytes 27983876 | tf_op jit(solution)/shard_map/while/body/eval_jaxpr/ikgd,jkd->kgij/dot_general | solution.py:134
  186.9 2.8 bitcast_add_fusion.5
  189.7 3.3 fusion.112
  193.4 9.3 %fusion.110 = f32[4,512,256,8]{2,1,3,0:T(8,128)} fusion(bf16[256,4,8,128]{3,0,2,1:T(8,128)(2,1)S(1)} %get-tuple-element.893, bf16[2048,4,128]{2,0,1:T(8,128)(2,1)} %get-tuple-element.889, s32[]{:T(128)S(6)} %select_n.137), kind=kOutput, calls=%fused_computation.31.clone.1 | convolution fusion | flops 1073741824 | bytes 19398660 | tf_op jit(solution)/shard_map/while/body/eval_jaxpr/ikgd,jkd->kgij/dot_general | solution.py:129
  202.7 8.7 %fusion.113 = f32[2048,4,128]{2,0,1:T(8,128)} fusion(f32[2048,4,128]{2,0,1:T(8,128)} %get-tuple-element.870, s32[]{:T(128)S(6)} %select_n.137, bf16[256,4,8,128]{3,0,2,1:T(8,128)(2,1)S(1)} %copy-done.6, f32[4,512,256,8]{2,1,3,0:T(8,128)} %fusion.110, f32[4,8,256]{2,1,0:T(8,128)S(1)} %bitcast.272, pred[256,512]{0,1:T(8,128)(4,1)S(1)} %compare_and_fusion.5), kind=kOutput, calls=%fused_computation.26.clone.1 | convolution fusion | flops 1094713344 | bytes 20086788 | tf_op jit(solution)/shard_map/while/body/eval_jaxpr/kgij,ikgd->jkd/dot_general | solution.py:145
  211.4 9.4 %fusion.111 = bf16[4,8,256,512]{2,3,1,0:T(8,128)(2,1)S(1)} fusion(f32[4,512,256,8]{2,1,3,0:T(8,128)} %fusion.110, bf16[256,4,8,128]{3,0,2,1:T(8,128)(2,1)} %get-tuple-element.896, f32[4,8,256]{2,1,0:T(8,128)S(1)} %bitcast.271, f32[4,8,256]{2,1,0:T(8,128)S(1)} %bitcast.273, pred[256,512]{0,1:T(8,128)(4,1)S(1)} %compare_and_fusion.5, ...), kind=kOutput, calls=%fused_computation.16.clone.1 | convolution fusion | flops 1103101952 | bytes 27983876 | tf_op jit(solution)/shard_map/while/body/eval_jaxpr/ikgd,jkd->kgij/dot_general | solution.py:134
  220.9 2.8 bitcast_add_fusion.5
  223.7 3.3 fusion.112
  227.4 9.3 %fusion.110 = f32[4,512,256,8]{2,1,3,0:T(8,128)} fusion(bf16[256,4,8,128]{3,0,2,1:T(8,128)(2,1)S(1)} %get-tuple-element.893, bf16[2048,4,128]{2,0,1:T(8,128)(2,1)} %get-tuple-element.889, s32[]{:T(128)S(6)} %select_n.137), kind=kOutput, calls=%fused_computation.31.clone.1 | convolution fusion | flops 1073741824 | bytes 19398660 | tf_op jit(solution)/shard_map/while/body/eval_jaxpr/ikgd,jkd->kgij/dot_general | solution.py:129
  236.7 8.7 %fusion.113 = f32[2048,4,128]{2,0,1:T(8,128)} fusion(f32[2048,4,128]{2,0,1:T(8,128)} %get-tuple-element.870, s32[]{:T(128)S(6)} %select_n.137, bf16[256,4,8,128]{3,0,2,1:T(8,128)(2,1)S(1)} %copy-done.6, f32[4,512,256,8]{2,1,3,0:T(8,128)} %fusion.110, f32[4,8,256]{2,1,0:T(8,128)S(1)} %bitcast.272, pred[256,512]{0,1:T(8,128)(4,1)S(1)} %compare_and_fusion.5), kind=kOutput, calls=%fused_computation.26.clone.1 | convolution fusion | flops 1094713344 | bytes 20086788 | tf_op jit(solution)/shard_map/while/body/eval_jaxpr/kgij,ikgd->jkd/dot_general | solution.py:145
  245.5 9.5 %fusion.111 = bf16[4,8,256,512]{2,3,1,0:T(8,128)(2,1)S(1)} fusion(f32[4,512,256,8]{2,1,3,0:T(8,128)} %fusion.110, bf16[256,4,8,128]{3,0,2,1:T(8,128)(2,1)} %get-tuple-element.896, f32[4,8,256]{2,1,0:T(8,128)S(1)} %bitcast.271, f32[4,8,256]{2,1,0:T(8,128)S(1)} %bitcast.273, pred[256,512]{0,1:T(8,128)(4,1)S(1)} %compare_and_fusion.5, ...), kind=kOutput, calls=%fused_computation.16.clone.1 | convolution fusion | flops 1103101952 | bytes 27983876 | tf_op jit(solution)/shard_map/while/body/eval_jaxpr/ikgd,jkd->kgij/dot_general | solution.py:134
  257.8 3.3 fusion.112
  261.5 9.3 %fusion.110 = f32[4,512,256,8]{2,1,3,0:T(8,128)} fusion(bf16[256,4,8,128]{3,0,2,1:T(8,128)(2,1)S(1)} %get-tuple-element.893, bf16[2048,4,128]{2,0,1:T(8,128)(2,1)} %get-tuple-element.889, s32[]{:T(128)S(6)} %select_n.137), kind=kOutput, calls=%fused_computation.31.clone.1 | convolution fusion | flops 1073741824 | bytes 19398660 | tf_op jit(solution)/shard_map/while/body/eval_jaxpr/ikgd,jkd->kgij/dot_general | solution.py:129
  270.8 8.7 %fusion.113 = f32[2048,4,128]{2,0,1:T(8,128)} fusion(f32[2048,4,128]{2,0,1:T(8,128)} %get-tuple-element.870, s32[]{:T(128)S(6)} %select_n.137, bf16[256,4,8,128]{3,0,2,1:T(8,128)(2,1)S(1)} %copy-done.6, f32[4,512,256,8]{2,1,3,0:T(8,128)} %fusion.110, f32[4,8,256]{2,1,0:T(8,128)S(1)} %bitcast.272, pred[256,512]{0,1:T(8,128)(4,1)S(1)} %compare_and_fusion.5), kind=kOutput, calls=%fused_computation.26.clone.1 | convolution fusion | flops 1094713344 | bytes 20086788 | tf_op jit(solution)/shard_map/while/body/eval_jaxpr/kgij,ikgd->jkd/dot_general | solution.py:145
  279.5 9.5 %fusion.111 = bf16[4,8,256,512]{2,3,1,0:T(8,128)(2,1)S(1)} fusion(f32[4,512,256,8]{2,1,3,0:T(8,128)} %fusion.110, bf16[256,4,8,128]{3,0,2,1:T(8,128)(2,1)} %get-tuple-element.896, f32[4,8,256]{2,1,0:T(8,128)S(1)} %bitcast.271, f32[4,8,256]{2,1,0:T(8,128)S(1)} %bitcast.273, pred[256,512]{0,1:T(8,128)(4,1)S(1)} %compare_and_fusion.5, ...), kind=kOutput, calls=%fused_computation.16.clone.1 | convolution fusion | flops 1103101952 | bytes 27983876 | tf_op jit(solution)/shard_map/while/body/eval_jaxpr/ikgd,jkd->kgij/dot_general | solution.py:134
  291.8 3.3 fusion.112
  295.2 5.2 %fusion.53 = (f32[2,256,4,128]{3,1,2,0:T(8,128)S(1)}, f32[2,256,4,128]{3,1,2,0:T(8,128)S(1)}, f32[2,256,4,128]{3,1,2,0:T(8,128)}, f32[2,256,4,128]{3,1,2,0:T(8,1...) fusion(f32[1,8,256,4,128]{4,2,1,3,0:T(8,128)} %bitcast.242, ...), kind=kLoop, calls=%fused_computation.75 | loop fusion | flops 1835008 | bytes 15728640 | tf_op jit(solution)/shard_map/squeeze | solution.py:167
  300.4 4.7 collective-permute-start.7
  305.1 3.6 collective-permute-start.8
  313.7 4.5 collective-permute-start.11
  318.1 41.8 %collective-permute-done.7 = f32[2,256,4,128]{3,1,2,0:T(8,128)S(1)} collective-permute-done((f32[2,256,4,128]{3,1,2,0:T(8,128)S(1)}, f32[2,256,4,128]{3,1,2,0:T(8,128)S(1)}, u32[]{:S(2)}, u32[]{:S(2)}) %collective-permute-start.7) | collective-permute-done | bytes 1048608 | tf_op jit(solution)/shard_map/ppermute | solution.py:15
  361.9 11.0 %collective-permute-start.12 = (f32[2,256,4,128]{3,1,2,0:T(8,128)}, f32[2,256,4,128]{3,1,2,0:T(8,128)}, u32[]{:S(2)}, u32[]{:S(2)}) collective-permute-start(f32[2,256,4,128]{3,1,2,0:T(8,128)} %get-tuple-element.659), channel_id=1, source_target_pairs={{12,0},{14,2},{16,4},{18,6},{20,8},{22,10},{24,12},{26,14},{28,16}... | collective-permute-start | bytes 3145736 | tf_op jit(solution)/shard_map/ppermute | solution.py:15
  373.2 3.3 copy.185
  376.4 10.5 %all_to_all.120 = bf16[256,32,128]{2,1,0:T(8,128)(2,1)S(1)} all-to-all(bf16[256,32,128]{2,1,0:T(8,128)(2,1)} %bitcast.251), channel_id=1, replica_groups=mesh['ctx'=64,'tp'=2] {'tp'}, dimensions={0} | all-to-all | bytes 4194304 | tf_op jit(solution)/shard_map/all_to_all | solution.py:172
  387.0 2.9 copy.186
  389.9 4.2 copy.200
  394.1 10.4 %collective-permute-done.11 = f32[2,256,4,128]{3,1,2,0:T(8,128)} collective-permute-done((f32[2,256,4,128]{3,1,2,0:T(8,128)}, f32[2,256,4,128]{3,1,2,0:T(8,128)}, u32[]{:S(2)}, u32[]{:S(2)}) %collective-permute-start.11) | collective-permute-done | bytes 1048608 | tf_op jit(solution)/shard_map/ppermute | solution.py:15
  404.5 61.3 %collective-permute-done.12 = f32[2,256,4,128]{3,1,2,0:T(8,128)} collective-permute-done((f32[2,256,4,128]{3,1,2,0:T(8,128)}, f32[2,256,4,128]{3,1,2,0:T(8,128)}, u32[]{:S(2)}, u32[]{:S(2)}) %collective-permute-start.12) | collective-permute-done | bytes 1048608 | tf_op jit(solution)/shard_map/ppermute | solution.py:15
  465.8 3.3 fusion.63
  469.4 5.2 %all_to_all.121 = bf16[256,4,128]{2,1,0:T(4,128)(2,1)S(1)} all-to-all(bf16[256,4,128]{2,1,0:T(4,128)(2,1)S(1)} %copy.197), channel_id=1, replica_groups=mesh['ctx'=64,'tp'=2] {'tp'}, dimensions={0} | all-to-all | bytes 524288 | tf_op jit(solution)/shard_map/all_to_all | solution.py:174
  475.8 3.9 all_to_all.122
  (151 shorter events, 50.1 us)
Async XLA Ops:
  2.6 6.1 %all-to-all-start = ((bf16[128,8,128]{2,0,1:T(8,128)(2,1)}), bf16[128,8,128]{2,0,1:T(8,128)(2,1)S(1)}, u32[]{:S(2)}, u32[]{:S(2)}) async-start(bf16[128,8,128]{2,0,1:T(8,128)(2,1)} %copy.163), calls=%async_computation | async-start | bytes 524288 | tf_op jit(solution)/shard_map/all_to_all | solution.py:52
  8.7 4.7 all-to-all-start.1
  14.3 85.8 %collective-permute-start.4 = (bf16[2,1,256,4,128]{4,2,3,0,1:T(8,128)(2,1)}, bf16[2,1,256,4,128]{4,2,3,0,1:T(8,128)(2,1)}, u32[]{:S(2)}, u32[]{:S(2)}) collective-permute-start(bf16[2,1,256,4,128]{4,2,3,0,1:T(8,128)(2,1)} %maximum_bitcast_fusion), channel_id=1, source_target_pairs={{0,10},{2,12},{4,14},{6,16},{8,18},{10,20},{12,22},{14,24},{16,26}... | collective-permute-start | bytes 1572872 | tf_op jit(solution)/shard_map/ppermute | solution.py:15
  18.4 80.6 %collective-permute-start.3 = (bf16[2,1,256,4,128]{4,2,3,0,1:T(8,128)(2,1)}, bf16[2,1,256,4,128]{4,2,3,0,1:T(8,128)(2,1)}, u32[]{:S(2)}, u32[]{:S(2)}) collective-permute-start(bf16[2,1,256,4,128]{4,2,3,0,1:T(8,128)(2,1)} %maximum_bitcast_fusion), channel_id=1, source_target_pairs={{0,8},{2,10},{4,12},{6,14},{8,16},{10,18},{12,20},{14,22},{16,24},... | collective-permute-start | bytes 1572872 | tf_op jit(solution)/shard_map/ppermute | solution.py:15
  21.6 76.2 %collective-permute-start.2 = (bf16[2,1,256,4,128]{4,2,3,0,1:T(8,128)(2,1)}, bf16[2,1,256,4,128]{4,2,3,0,1:T(8,128)(2,1)}, u32[]{:S(2)}, u32[]{:S(2)}) collective-permute-start(bf16[2,1,256,4,128]{4,2,3,0,1:T(8,128)(2,1)} %maximum_bitcast_fusion), channel_id=1, source_target_pairs={{0,6},{2,8},{4,10},{6,12},{8,14},{10,16},{12,18},{14,20},{16,22},{... | collective-permute-start | bytes 1572872 | tf_op jit(solution)/shard_map/ppermute | solution.py:15
  25.7 65.9 %collective-permute-start.1 = (bf16[2,1,256,4,128]{4,2,3,0,1:T(8,128)(2,1)}, bf16[2,1,256,4,128]{4,2,3,0,1:T(8,128)(2,1)}, u32[]{:S(2)}, u32[]{:S(2)}) collective-permute-start(bf16[2,1,256,4,128]{4,2,3,0,1:T(8,128)(2,1)} %maximum_bitcast_fusion), channel_id=1, source_target_pairs={{0,4},{2,6},{4,8},{6,10},{8,12},{10,14},{12,16},{14,18},{16,20},{1... | collective-permute-start | bytes 1572872 | tf_op jit(solution)/shard_map/ppermute | solution.py:15
  29.2 55.7 %collective-permute-start = (bf16[2,1,256,4,128]{4,2,3,0,1:T(8,128)(2,1)}, bf16[2,1,256,4,128]{4,2,3,0,1:T(8,128)(2,1)}, u32[]{:S(2)}, u32[]{:S(2)}) collective-permute-start(bf16[2,1,256,4,128]{4,2,3,0,1:T(8,128)(2,1)} %maximum_bitcast_fusion), channel_id=1, source_target_pairs={{0,2},{2,4},{4,6},{6,8},{8,10},{10,12},{12,14},{14,16},{16,18},{18... | collective-permute-start | bytes 1572872 | tf_op jit(solution)/shard_map/ppermute | solution.py:15
  34.6 8.4 %copy-start.9 = (s32[256]{0:T(256)S(1)}, s32[256]{0:T(256)}, u32[]{:S(2)}) copy-start(s32[256]{0:T(256)} %param.15) | copy-start | bytes 3076
  37.5 22.4 %all-to-all-start.4 = ((bf16[128,64,128]{2,0,1:T(8,128)(2,1)}), bf16[128,64,128]{2,0,1:T(8,128)(2,1)S(1)}, u32[]{:S(2)}, u32[]{:S(2)}) async-start(bf16[128,64,128]{2,0,1:T(8,128)(2,1)} %copy.180), calls=%async_computation.4 | async-start | bytes 4194304 | tf_op jit(solution)/shard_map/all_to_all | solution.py:45
  60.0 7.6 %all-to-all-start.3 = ((bf16[128,64,128]{2,0,1:T(8,128)(2,1)}), bf16[128,64,128]{2,0,1:T(8,128)(2,1)}, u32[]{:S(2)}, u32[]{:S(2)}) async-start(bf16[128,64,128]{2,0,1:T(8,128)(2,1)} %copy.176), calls=%async_computation.3 | async-start | bytes 4194304 | tf_op jit(solution)/shard_map/all_to_all | solution.py:38
  67.5 11.1 %all-to-all-start.2 = ((bf16[128,64,128]{2,0,1:T(8,128)(2,1)}), bf16[128,64,128]{2,0,1:T(8,128)(2,1)S(1)}, u32[]{:S(2)}, u32[]{:S(2)}) async-start(bf16[128,64,128]{2,0,1:T(8,128)(2,1)} %copy.170), calls=%async_computation.2 | async-start | bytes 4194304 | tf_op jit(solution)/shard_map/all_to_all | solution.py:31
  71.6 4.4 copy-start.4
  74.7 1.3 copy-start.3
  81.0 9.5 %copy-start.5 = (bf16[2,8,256,4,128]{4,2,3,0,1:T(8,128)(2,1)S(1)}, bf16[2,8,256,4,128]{4,2,3,0,1:T(8,128)(2,1)}, u32[]{:S(2)}) copy-start(bf16[2,8,256,4,128]{4,2,3,0,1:T(8,128)(2,1)} %constant_dynamic-update-slice_fusion.7) | copy-start | bytes 12582916
  84.9 20.4 %collective-permute-start.5 = (bf16[2,1,256,4,128]{4,2,3,0,1:T(8,128)(2,1)}, bf16[2,1,256,4,128]{4,2,3,0,1:T(8,128)(2,1)S(1)}, u32[]{:S(2)}, u32[]{:S(2)}) collective-permute-start(bf16[2,1,256,4,128]{4,2,3,0,1:T(8,128)(2,1)} %maximum_bitcast_fusion), channel_id=1, source_target_pairs={{0,12},{2,14},{4,16},{6,18},{8,20},{10,22},{12,24},{14,26},{16,28}... | collective-permute-start | bytes 1572872 | tf_op jit(solution)/shard_map/ppermute | solution.py:15
  91.6 25.6 %collective-permute-start.6 = (bf16[2,1,256,4,128]{4,2,3,0,1:T(8,128)(2,1)}, bf16[2,1,256,4,128]{4,2,3,0,1:T(8,128)(2,1)S(1)}, u32[]{:S(2)}, u32[]{:S(2)}) collective-permute-start(bf16[2,1,256,4,128]{4,2,3,0,1:T(8,128)(2,1)} %maximum_bitcast_fusion), channel_id=1, source_target_pairs={{0,14},{2,16},{4,18},{6,20},{8,22},{10,24},{12,26},{14,28},{16,30}... | collective-permute-start | bytes 1572872 | tf_op jit(solution)/shard_map/ppermute | solution.py:15
  159.3 9.3 %copy-start.6 = (bf16[256,4,8,128]{3,0,2,1:T(8,128)(2,1)S(1)}, bf16[256,4,8,128]{3,0,2,1:T(8,128)(2,1)}, u32[]{:S(2)}) copy-start(bf16[256,4,8,128]{3,0,2,1:T(8,128)(2,1)} %get-tuple-element.896) | copy-start | bytes 6291460 | tf_op jit(solution)/shard_map/while
  177.4 9.5 %copy-start = (f32[256,4,8,128]{0,3,2,1:T(8,128)S(1)}, f32[256,4,8,128]{0,3,2,1:T(8,128)}, u32[]{:S(2)}) copy-start(f32[256,4,8,128]{0,3,2,1:T(8,128)} %get-tuple-element.868) | copy-start | bytes 12582916 | tf_op jit(solution)/shard_map/while
  189.7 3.3 copy-start.1
  193.4 9.3 %copy-start.6 = (bf16[256,4,8,128]{3,0,2,1:T(8,128)(2,1)S(1)}, bf16[256,4,8,128]{3,0,2,1:T(8,128)(2,1)}, u32[]{:S(2)}) copy-start(bf16[256,4,8,128]{3,0,2,1:T(8,128)(2,1)} %get-tuple-element.896) | copy-start | bytes 6291460 | tf_op jit(solution)/shard_map/while
  211.4 9.5 %copy-start = (f32[256,4,8,128]{0,3,2,1:T(8,128)S(1)}, f32[256,4,8,128]{0,3,2,1:T(8,128)}, u32[]{:S(2)}) copy-start(f32[256,4,8,128]{0,3,2,1:T(8,128)} %get-tuple-element.868) | copy-start | bytes 12582916 | tf_op jit(solution)/shard_map/while
  223.7 3.3 copy-start.1
  227.4 9.3 %copy-start.6 = (bf16[256,4,8,128]{3,0,2,1:T(8,128)(2,1)S(1)}, bf16[256,4,8,128]{3,0,2,1:T(8,128)(2,1)}, u32[]{:S(2)}) copy-start(bf16[256,4,8,128]{3,0,2,1:T(8,128)(2,1)} %get-tuple-element.896) | copy-start | bytes 6291460 | tf_op jit(solution)/shard_map/while
  245.4 9.5 %copy-start = (f32[256,4,8,128]{0,3,2,1:T(8,128)S(1)}, f32[256,4,8,128]{0,3,2,1:T(8,128)}, u32[]{:S(2)}) copy-start(f32[256,4,8,128]{0,3,2,1:T(8,128)} %get-tuple-element.868) | copy-start | bytes 12582916 | tf_op jit(solution)/shard_map/while
  257.8 3.4 copy-start.1
  261.5 9.3 %copy-start.6 = (bf16[256,4,8,128]{3,0,2,1:T(8,128)(2,1)S(1)}, bf16[256,4,8,128]{3,0,2,1:T(8,128)(2,1)}, u32[]{:S(2)}) copy-start(bf16[256,4,8,128]{3,0,2,1:T(8,128)(2,1)} %get-tuple-element.896) | copy-start | bytes 6291460 | tf_op jit(solution)/shard_map/while
  279.5 9.5 %copy-start = (f32[256,4,8,128]{0,3,2,1:T(8,128)S(1)}, f32[256,4,8,128]{0,3,2,1:T(8,128)}, u32[]{:S(2)}) copy-start(f32[256,4,8,128]{0,3,2,1:T(8,128)} %get-tuple-element.868) | copy-start | bytes 12582916 | tf_op jit(solution)/shard_map/while
  291.8 3.3 copy-start.1
  295.1 77.7 %copy-start.2 = (f32[256,4,8,128]{0,3,2,1:T(8,128)S(1)}, f32[256,4,8,128]{0,3,2,1:T(8,128)}, u32[]{:S(2)}) copy-start(f32[256,4,8,128]{0,3,2,1:T(8,128)} %get-tuple-element.391) | copy-start | bytes 12582916
  300.4 59.6 %collective-permute-start.7 = (f32[2,256,4,128]{3,1,2,0:T(8,128)S(1)}, f32[2,256,4,128]{3,1,2,0:T(8,128)S(1)}, u32[]{:S(2)}, u32[]{:S(2)}) collective-permute-start(f32[2,256,4,128]{3,1,2,0:T(8,128)S(1)} %get-tuple-element.653), channel_id=1, source_target_pairs={{2,0},{4,2},{6,4},{8,6},{10,8},{12,10},{14,12},{16,14},{18,16},{20... | collective-permute-start | bytes 3145736 | tf_op jit(solution)/shard_map/ppermute | solution.py:15
  305.1 56.8 %collective-permute-start.8 = (f32[2,256,4,128]{3,1,2,0:T(8,128)S(1)}, f32[2,256,4,128]{3,1,2,0:T(8,128)S(1)}, u32[]{:S(2)}, u32[]{:S(2)}) collective-permute-start(f32[2,256,4,128]{3,1,2,0:T(8,128)S(1)} %get-tuple-element.654), channel_id=1, source_target_pairs={{4,0},{6,2},{8,4},{10,6},{12,8},{14,10},{16,12},{18,14},{20,16},{2... | collective-permute-start | bytes 3145736 | tf_op jit(solution)/shard_map/ppermute | solution.py:15
  308.7 85.4 %collective-permute-start.9 = (f32[2,256,4,128]{3,1,2,0:T(8,128)}, f32[2,256,4,128]{3,1,2,0:T(8,128)}, u32[]{:S(2)}, u32[]{:S(2)}) collective-permute-start(f32[2,256,4,128]{3,1,2,0:T(8,128)} %get-tuple-element.655), channel_id=1, source_target_pairs={{6,0},{8,2},{10,4},{12,6},{14,8},{16,10},{18,12},{20,14},{22,16},{... | collective-permute-start | bytes 3145736 | tf_op jit(solution)/shard_map/ppermute | solution.py:15
  310.8 83.3 %collective-permute-start.10 = (f32[2,256,4,128]{3,1,2,0:T(8,128)}, f32[2,256,4,128]{3,1,2,0:T(8,128)}, u32[]{:S(2)}, u32[]{:S(2)}) collective-permute-start(f32[2,256,4,128]{3,1,2,0:T(8,128)} %get-tuple-element.656), channel_id=1, source_target_pairs={{8,0},{10,2},{12,4},{14,6},{16,8},{18,10},{20,12},{22,14},{24,16},... | collective-permute-start | bytes 3145736 | tf_op jit(solution)/shard_map/ppermute | solution.py:15
  313.7 90.8 %collective-permute-start.11 = (f32[2,256,4,128]{3,1,2,0:T(8,128)}, f32[2,256,4,128]{3,1,2,0:T(8,128)}, u32[]{:S(2)}, u32[]{:S(2)}) collective-permute-start(f32[2,256,4,128]{3,1,2,0:T(8,128)} %get-tuple-element.657), channel_id=1, source_target_pairs={{10,0},{12,2},{14,4},{16,6},{18,8},{20,10},{22,12},{24,14},{26,16}... | collective-permute-start | bytes 3145736 | tf_op jit(solution)/shard_map/ppermute | solution.py:15
  359.9 44.5 %collective-permute-start.13 = (f32[2,256,4,128]{3,1,2,0:T(8,128)}, f32[2,256,4,128]{3,1,2,0:T(8,128)}, u32[]{:S(2)}, u32[]{:S(2)}) collective-permute-start(f32[2,256,4,128]{3,1,2,0:T(8,128)} %get-tuple-element.658), channel_id=1, source_target_pairs={{14,0},{16,2},{18,4},{20,6},{22,8},{24,10},{26,12},{28,14},{30,16}... | collective-permute-start | bytes 3145736 | tf_op jit(solution)/shard_map/ppermute | solution.py:15
  361.9 11.0 %copy-start.7 = (f32[2,256,4,128]{3,1,2,0:T(8,128)}, f32[2,256,4,128]{3,1,2,0:T(8,128)S(1)}, u32[]{:S(2)}) copy-start(f32[2,256,4,128]{3,1,2,0:T(8,128)S(1)} %collective-permute-done.8) | copy-start | bytes 3145732
  361.9 103.9 %collective-permute-start.12 = (f32[2,256,4,128]{3,1,2,0:T(8,128)}, f32[2,256,4,128]{3,1,2,0:T(8,128)}, u32[]{:S(2)}, u32[]{:S(2)}) collective-permute-start(f32[2,256,4,128]{3,1,2,0:T(8,128)} %get-tuple-element.659), channel_id=1, source_target_pairs={{12,0},{14,2},{16,4},{18,6},{20,8},{22,10},{24,12},{26,14},{28,16}... | collective-permute-start | bytes 3145736 | tf_op jit(solution)/shard_map/ppermute | solution.py:15
  389.9 75.9 %copy-start.8 = (f32[2,256,4,128]{3,1,2,0:T(8,128)S(1)}, f32[2,256,4,128]{3,1,2,0:T(8,128)}, u32[]{:S(2)}) copy-start(f32[2,256,4,128]{3,1,2,0:T(8,128)} %copy-done.7) | copy-start | bytes 3145732
where the time goes:
time: 483 us; the launch traced here: 481 us
  matrix products  149 us (31%)
  waiting for transfers between devices  131 us (27%)
  starting transfers between devices  80.3 us (17%)
  local copies, waits for them, and re-layouts  67.4 us (14%)
  other arithmetic  32 us (7%)
  blocking collectives  19.7 us (4%)
    ppermute x14, waiting for transfers between devices, from_behind(): return lax.ppermute(x, axis, pairs)  129 us
    ppermute x14, starting transfers between devices, from_behind(): return lax.ppermute(x, axis, pairs)  58.4 us
    dot_general x4, matrix products, grad_update(): jnp.einsum('ikgd,jkd->kgij', g_loc, v_blk, preferred_element_type=jnp.flo...  37.8 us
    dot_general x4, matrix products, grad_update(): jnp.einsum('ikgd,jkd->kgij', q_loc, k_blk, preferred_element_type=jnp.flo...  37.2 us
    dot_general x4, matrix products, grad_update(): jnp.einsum('kgij,ikgd->jkd', probs_low, g_loc, preferred_element_type=jnp...  34.9 us
    unnamed x30, local copies, waits for them, and re-layouts  30.5 us
    reduce_sum x4, other arithmetic, stats_update(): jnp.sum(jnp.where(allowed, jnp.exp(masked - new_top), 0.0), axis=-1, keep...  16.8 us
    dot_general x4, matrix products, stats_update(): jnp.einsum('ikgd,jkd->kgij', q_loc, k_blk, preferred_element_type=jnp.flo...  14.9 us
  transfers between devices with their start and end apart: 19, of which 6 were waited for; matrix products, arithmetic and copies ran while one was open for 12% of the time, Pallas kernels for 0%

commit v1 on v0

v1 whole, which is shorter than its diff:
```python
import functools
import math

import jax
import jax.numpy as jnp
from jax import lax
from jax.experimental import pallas as pl
from jax.experimental.pallas import tpu as pltpu
from jax.sharding import PartitionSpec as P

HEAD_SIZE = 128
SHARD = 256
HALF = 128
SLOTS = 8
ROW = 4
NEG = -1e30
MESH = pl.DeviceIdType.MESH
F32 = jnp.float32
BF16 = jnp.bfloat16


def dot_nt(a, b):
    return lax.dot_general(a, b, (((1,), (1,)), ((), ())), preferred_element_type=F32)


def dot_nn(a, b):
    return jnp.dot(a, b, preferred_element_type=F32)


def kernel(
    n_ctx,
    n_kv,
    width,
    q_in,
    k_in,
    v_in,
    o_in,
    g_in,
    len_ref,
    dq_out,
    dk_out,
    dv_out,
    qgo,
    kv,
    ebuf,
    bias,
    mx,
    zs,
    delta,
    dqt,
    acc,
    ret_out,
    ret_in,
    dq_stage,
    dkv_stage,
    sem_qgo_l,
    sem_qgo_s,
    sem_qgo_r,
    sem_kv0_l,
    sem_kv0_s,
    sem_kv0_r,
    sem_kv_s,
    sem_kv_r,
    sem_ret_s,
    sem_ret_r,
    sem_dq_l,
    sem_dq_s,
    sem_dq_r,
    sem_dkv_l,
    sem_dkv_s,
    sem_dkv_r,
):
    ctx = lax.axis_index("ctx")
    tp = lax.axis_index("tp")
    x = lax.rem(ctx, ROW)
    row = ctx - x
    other = 1 - tp
    up = lax.rem(ctx + ROW, n_ctx)
    down = lax.rem(ctx + n_ctx - ROW, n_ctx)
    wide = width * HEAD_SIZE
    inv_root = HEAD_SIZE ** -0.5
    to_exp2 = inv_root * math.log2(math.e)

    def along(d):
        return row + lax.rem(x + d, ROW)

    barrier = pltpu.get_barrier_semaphore()
    for peer in [(ctx, other), (up, tp), (down, tp)] + [(along(d), tp) for d in (1, 2, 3)]:
        pl.semaphore_signal(barrier, inc=1, device_id=peer, device_id_type=MESH)
    pl.semaphore_wait(barrier, 6)

    def cols(head, size):
        return pl.ds(pl.multiple_of(head * size, size), size)

    mine = pl.ds(pl.multiple_of(tp * HALF, HALF), HALF)
    theirs = pl.ds(pl.multiple_of(other * HALF, HALF), HALF)
    wides = (q_in, g_in, o_in)
    narrows = (k_in, v_in)

    def wide_local(a, g):
        return pltpu.make_async_copy(
            wides[a].at[:, cols(tp * n_kv + g, wide)], qgo.at[a, g, mine], sem_qgo_l.at[a, g])

    def wide_remote(a, g):
        return pltpu.make_async_remote_copy(
            wides[a].at[:, cols(other * n_kv + g, wide)], qgo.at[a, g, mine],
            sem_qgo_s.at[a, g], sem_qgo_r.at[a, g], device_id=(ctx, other), device_id_type=MESH)

    def narrow_local(a, g):
        return pltpu.make_async_copy(
            narrows[a].at[:, cols(tp * n_kv + g, HEAD_SIZE)], kv.at[a, g, 0, mine], sem_kv0_l.at[a, g])

    def narrow_remote(a, g):
        return pltpu.make_async_remote_copy(
            narrows[a].at[:, cols(other * n_kv + g, HEAD_SIZE)], kv.at[a, g, 0, mine],
            sem_kv0_s.at[a, g], sem_kv0_r.at[a, g], device_id=(ctx, other), device_id_type=MESH)

    def kv_y(a, g, d):
        return pltpu.make_async_remote_copy(
            kv.at[a, g, d], kv.at[a, g, ROW + d],
            sem_kv_s.at[a, g, ROW + d], sem_kv_r.at[a, g, ROW + d], device_id=(up, tp), device_id_type=MESH)

    def kv_x(a, g, d):
        held = ROW * ((x + d) // ROW)
        return pltpu.make_async_remote_copy(
            kv.at[a, g, held], kv.at[a, g, d],
            sem_kv_s.at[a, g, d], sem_kv_r.at[a, g, d], device_id=(along(d), tp), device_id_type=MESH)

    def ret_y(g, slot):
        return pltpu.make_async_remote_copy(
            ret_out.at[g, slot], ret_in.at[g, slot],
            sem_ret_s.at[g, slot], sem_ret_r.at[g, slot], device_id=(down, tp), device_id_type=MESH)

    def ret_x(g, d):
        return pltpu.make_async_remote_copy(
            ret_out.at[g, d], ret_in.at[g, d],
            sem_ret_s.at[g, d], sem_ret_r.at[g, d], device_id=(along(ROW - d), tp), device_id_type=MESH)

    def dq_local(g):
        return pltpu.make_async_copy(
            dq_stage.at[g, mine], dq_out.at[:, cols(tp * n_kv + g, wide)], sem_dq_l.at[g])

    def dq_remote(g):
        return pltpu.make_async_remote_copy(
            dq_stage.at[g, theirs], dq_out.at[:, cols(tp * n_kv + g, wide)],
            sem_dq_s.at[g], sem_dq_r.at[g], device_id=(ctx, other), device_id_type=MESH)

    dkvs = (dk_out, dv_out)

    def dkv_local(a, g):
        return pltpu.make_async_copy(
            dkv_stage.at[g, a, mine], dkvs[a].at[:, cols(tp * n_kv + g, HEAD_SIZE)], sem_dkv_l.at[a, g])

    def dkv_remote(a, g):
        return pltpu.make_async_remote_copy(
            dkv_stage.at[g, a, theirs], dkvs[a].at[:, cols(tp * n_kv + g, HEAD_SIZE)],
            sem_dkv_s.at[a, g], sem_dkv_r.at[a, g], device_id=(ctx, other), device_id_type=MESH)

    for g in range(n_kv):
        for a in (0, 1):
            narrow_remote(a, g).start()
            narrow_local(a, g).start()
        if g == 0:
            wide_remote(0, 0).start()
            wide_local(0, 0).start()
    for g in range(n_kv):
        for a in (0, 1, 2):
            if (a, g) != (0, 0):
                wide_remote(a, g).start()
                wide_local(a, g).start()

    first = (ctx * SHARD).astype(F32)
    docs = len_ref.shape[1]
    lens = len_ref[...].astype(F32)
    r_d = lax.broadcasted_iota(jnp.int32, (docs, docs), 0)
    c_d = lax.broadcasted_iota(jnp.int32, (docs, docs), 1)
    starts = jnp.sum(jnp.where(c_d < r_d, jnp.broadcast_to(lens, (docs, docs)), 0.0), axis=1, keepdims=True)
    pos = lax.broadcasted_iota(jnp.int32, (docs, SHARD), 1).astype(F32) + first
    begin = jnp.max(jnp.where(starts <= pos, jnp.broadcast_to(starts, (docs, SHARD)), 0.0), axis=0, keepdims=True)
    q_row = lax.broadcasted_iota(jnp.int32, (SHARD, SHARD), 1).astype(F32) + first
    k_row = lax.broadcasted_iota(jnp.int32, (SHARD, SHARD), 0).astype(F32) + first

    def write_bias(s, carry):
        k_pos = k_row - (s * SHARD).astype(F32)
        keep = (k_pos >= begin) & (k_pos <= q_row)
        bias[s] = jnp.where(keep, 0.0, NEG)
        return carry

    lax.fori_loop(0, SLOTS, write_bias, 0)

    for g in range(n_kv):
        for a in (0, 1):
            narrow_local(a, g).wait()
            narrow_remote(a, g).wait_recv()
            kv_y(a, g, 0).start()

    def forward_x(g):
        for a in (0, 1):
            kv_y(a, g, 0).wait_recv()
        for a in (0, 1):
            for d in (1, 2, 3):
                kv_x(a, g, d).start()

    def forward_y(g, d):
        for a in (0, 1):
            kv_x(a, g, d).wait_recv()
            kv_y(a, g, d).start()

    def back_x(g):
        par = lax.rem(g, 2)

        def one(d, carry):
            ret_y(g, ROW + d).wait_recv()
            ret_out[g, d] = (acc[par, d] + ret_in[g, ROW + d].astype(F32)).astype(BF16)
            ret_x(g, d).start()
            return carry

        lax.fori_loop(1, ROW, one, 0)

    def back_y(g):
        par = lax.rem(g, 2)
        far = acc[par, ROW]
        near = acc[par, 0]
        for d in (1, 2, 3):
            ret_x(g, d).wait_recv()
            part = ret_in[g, d].astype(F32)
            crosses = ((x + d) // ROW).astype(F32)
            far = far + part * crosses
            near = near + part * (1.0 - crosses)
        ret_out[g, ROW] = far.astype(BF16)
        ret_y(g, ROW).start()
        acc[par, 0] = near

    def back_end(g):
        par = lax.rem(g, 2)
        ret_y(g, ROW).wait_recv()
        total = (acc[par, 0] + ret_in[g, ROW].astype(F32)).astype(BF16)
        dkv_stage[g] = total
        for a in (0, 1):
            dkv_remote(a, g).start()
            dkv_local(a, g).start()

    def head_cols(h):
        return slice(h * HEAD_SIZE, (h + 1) * HEAD_SIZE)

    def phase_a(g, s):
        keys = kv[0, g, s]
        tops, sums = [], []
        for h in range(width):
            sc = dot_nt(keys, qgo[0, g, :, head_cols(h)])
            sc = sc * to_exp2 + bias[s]
            top = jnp.max(sc, axis=0, keepdims=True)
            e = jnp.exp2(sc - top)
            ebuf[s, h] = e
            tops.append(top)
            sums.append(jnp.sum(e, axis=0, keepdims=True))
        mx[s] = jnp.concatenate(tops, axis=0)
        zs[s] = jnp.concatenate(sums, axis=0)

    def normalise(g):
        top = mx[0]
        for s in range(1, SLOTS):
            top = jnp.maximum(top, mx[s])
        total = jnp.zeros_like(top)
        for s in range(SLOTS):
            f = jnp.exp2(mx[s] - top)
            total = total + zs[s] * f
            mx[s] = f
        inv = 1.0 / total
        for s in range(SLOTS):
            mx[s] = mx[s] * inv
        ones = jnp.ones((8, 2 * HEAD_SIZE), BF16)
        for h in range(width):
            prod = qgo[1, g, :, head_cols(h)].astype(F32) * qgo[2, g, :, head_cols(h)].astype(F32)
            hi = prod.astype(BF16)
            lo = (prod - hi.astype(F32)).astype(BF16)
            delta[h : h + 1] = dot_nt(ones, jnp.concatenate([hi, lo], axis=1))[0:1]
        dqt[...] = jnp.zeros_like(dqt)

    def phase_b(g, s):
        keys = kv[0, g, s]
        values = kv[1, g, s]
        keys_t = keys.T
        f = mx[s]
        dk = jnp.zeros((SHARD, HEAD_SIZE), F32)
        dv = jnp.zeros((SHARD, HEAD_SIZE), F32)
        for h in range(width):
            q_h = qgo[0, g, :, head_cols(h)]
            g_h = qgo[1, g, :, head_cols(h)]
            p = ebuf[s, h] * f[h : h + 1]
            dp = dot_nt(values, g_h)
            ds = (p * (dp - delta[h : h + 1])).astype(BF16)
            dv = dv + dot_nn(p.astype(BF16), g_h)
            dk = dk + dot_nn(ds, q_h)
            dqt[h] += dot_nn(keys_t, ds)
        return dk * inv_root, dv

    def finish_dq(g):
        for h in range(width):
            dq_stage[g, :, head_cols(h)] = (dqt[h].T * inv_root).astype(BF16)
        dq_remote(g).start()
        dq_local(g).start()

    def head_step(g, carry):
        par = lax.rem(g, 2)
        wide_local(0, g).wait()
        wide_remote(0, g).wait_recv()

        def a_step(i, carry_a):
            s = lax.select(i == 0, 0, lax.select(i == 1, ROW, lax.select(i < 5, i - 1, i)))

            @pl.when((g == 0) & (i == 1))
            def _():
                forward_x(g)

            @pl.when((g == 0) & (i >= 2) & (i < 5))
            def _():
                forward_y(g, i - 1)

            @pl.when(i >= 5)
            def _():
                kv_y(0, g, i - ROW).wait_recv()

            @pl.when((g > 0) & (i == 5))
            def _():
                back_x(g - 1)

            phase_a(g, s)
            return carry_a

        lax.fori_loop(0, SLOTS, a_step, 0)

        for a in (1, 2):
            wide_local(a, g).wait()
            wide_remote(a, g).wait_recv()
        normalise(g)

        def b_step(i, carry_b):
            s = lax.select(i < 3, i + 5, lax.rem(i + 3, 5))

            @pl.when(i < 3)
            def _():
                kv_y(1, g, i + 1).wait_recv()

            @pl.when((g < n_kv - 1) & (i == 0))
            def _():
                forward_x(g + 1)

            @pl.when((g < n_kv - 1) & (i >= 3) & (i < 6))
            def _():
                forward_y(g + 1, i - 2)

            @pl.when((g > 0) & (i == 2))
            def _():
                back_y(g - 1)

            @pl.when((g > 0) & (i == 7))
            def _():
                back_end(g - 1)

            dk, dv = phase_b(g, s)

            @pl.when(i < 3)
            def _():
                ret_out[g, s, 0] = dk.astype(BF16)
                ret_out[g, s, 1] = dv.astype(BF16)
                ret_y(g, s).start()

            @pl.when(i >= 3)
            def _():
                acc[par, s, 0] = dk
                acc[par, s, 1] = dv

            return carry_b

        lax.fori_loop(0, SLOTS, b_step, 0)
        finish_dq(g)
        return carry

    lax.fori_loop(0, n_kv, head_step, 0)
    last = jnp.int32(n_kv - 1)
    back_x(last)
    back_y(last)
    back_end(last)

    def drain(g, carry):
        for a in (0, 1, 2):
            wide_remote(a, g).wait_send()
        for a in (0, 1):
            narrow_remote(a, g).wait_send()
            for d in range(ROW):
                kv_y(a, g, d).wait_send()
            for d in (1, 2, 3):
                kv_x(a, g, d).wait_send()
            dkv_local(a, g).wait()
            dkv_remote(a, g).wait()
        for s in range(ROW, SLOTS):
            ret_y(g, s).wait_send()
        for d in (1, 2, 3):
            ret_x(g, d).wait_send()
        dq_local(g).wait()
        dq_remote(g).wait()
        return carry

    lax.fori_loop(0, n_kv, drain, 0)


def per_device(queries, key_matrix, value_matrix, attention_output, output_gradient, lengths):
    n_ctx = lax.axis_size("ctx")
    n_tp = lax.axis_size("tp")
    heads_q = queries.shape[1] // HEAD_SIZE
    heads_kv = key_matrix.shape[1] // HEAD_SIZE
    n_kv = heads_kv // n_tp
    width = heads_q // heads_kv
    wide = width * HEAD_SIZE
    dma = pltpu.SemaphoreType.DMA
    flops = 5 * 2 * SHARD * SLOTS * SHARD * HEAD_SIZE * n_kv * width
    return pl.pallas_call(
        functools.partial(kernel, n_ctx, n_kv, width),
        out_shape=(
            jax.ShapeDtypeStruct(queries.shape, BF16),
            jax.ShapeDtypeStruct(key_matrix.shape, BF16),
            jax.ShapeDtypeStruct(value_matrix.shape, BF16),
        ),
        in_specs=[pl.BlockSpec(memory_space=pl.ANY)] * 5 + [pl.BlockSpec(memory_space=pltpu.VMEM)],
        out_specs=(pl.BlockSpec(memory_space=pl.ANY),) * 3,
        scratch_shapes=[
            pltpu.VMEM((3, n_kv, SHARD, wide), BF16),
            pltpu.VMEM((2, n_kv, SLOTS, SHARD, HEAD_SIZE), BF16),
            pltpu.VMEM((SLOTS, width, SHARD, SHARD), F32),
            pltpu.VMEM((SLOTS, SHARD, SHARD), F32),
            pltpu.VMEM((SLOTS, width, SHARD), F32),
            pltpu.VMEM((SLOTS, width, SHARD), F32),
            pltpu.VMEM((width, SHARD), F32),
            pltpu.VMEM((width, HEAD_SIZE, SHARD), F32),
            pltpu.VMEM((2, ROW + 1, 2, SHARD, HEAD_SIZE), F32),
            pltpu.VMEM((n_kv, SLOTS, 2, SHARD, HEAD_SIZE), BF16),
            pltpu.VMEM((n_kv, SLOTS, 2, SHARD, HEAD_SIZE), BF16),
            pltpu.VMEM((n_kv, SHARD, wide), BF16),
            pltpu.VMEM((n_kv, 2, SHARD, HEAD_SIZE), BF16),
            dma((3, n_kv)),
            dma((3, n_kv)),
            dma((3, n_kv)),
            dma((2, n_kv)),
            dma((2, n_kv)),
            dma((2, n_kv)),
            dma((2, n_kv, SLOTS)),
            dma((2, n_kv, SLOTS)),
            dma((n_kv, SLOTS)),
            dma((n_kv, SLOTS)),
            dma((n_kv,)),
            dma((n_kv,)),
            dma((n_kv,)),
            dma((2, n_kv)),
            dma((2, n_kv)),
            dma((2, n_kv)),
        ],
        compiler_params=pltpu.CompilerParams(
            collective_id=0, has_side_effects=True, vmem_limit_bytes=60 * 1024 * 1024
        ),
        cost_estimate=pl.CostEstimate(
            flops=flops, bytes_accessed=10 * 1024 * 1024, transcendentals=flops // (10 * HEAD_SIZE)
        ),
        name="attention_backward",
    )(
        queries,
        key_matrix,
        value_matrix,
        attention_output,
        output_gradient,
        lengths.reshape(1, lengths.shape[0]),
    )


def solution(mesh):
    rows = P(("ctx", "tp"), None)
    return jax.shard_map(
        per_device,
        mesh=mesh,
        in_specs=(rows, rows, rows, rows, rows, P()),
        out_specs=(rows, rows, rows),
        check_vma=False,
    )
```

time: 483 us -> 145 us (0.30)
  the two profiles are of different devices: /device:TPU:65 before, /device:TPU:1 now
where the time goes in v1:
time: 145 us
  Pallas kernels  140 us (97%)
  local copies, waits for them, and re-layouts  4.56 us (3%)
    pallas_call x1, Pallas kernels, per_device(): pl.pallas_call(functools.partial(kernel, n_ctx, n_kv, width), out_shape=(...  140 us
    unnamed x7, local copies, waits for them, and re-layouts  4.56 us

profile of v1, /device:TPU:1, one launch (start us, length us, event | category | flops | bytes accessed | tf_op | source)
XLA Modules:
  0.0 144.9 jit_solution(7043998812070492245)
XLA Ops:
  0.6 139.7 %attention_backward.1 = (bf16[128,8192]{1,0:T(8,128)(2,1)}, bf16[128,1024]{1,0:T(8,128)(2,1)}, bf16[128,1024]{1,0:T(8,128)(2,1)}) custom-call(bf16[128,8192]{1,0:T(8,128)(2,1)} %q_in.1, bf16[128,1024]{1,0:T(8,128)(2,1)} %k_in.1, bf16[128,1024]{1,0:T(8,128)(2,1)} %v_in.1, bf16[128,8192]{1,0:T(8,128)(2,1)} %o_in.1, bf16[128,8192]{1,0:T(8,128)(2,1)} %g_in.1, ...), custom_call_target="tpu_custom_call" | custom-call | flops 21474836480 | bytes 10485760 | tf_op jit(solution)/shard_map/attention_backward/pallas_call | solution.py:418
  140.3 0.0 copy-start.1
  140.4 0.0 copy-start
  140.4 3.2 %copy.12 = bf16[128,8192]{1,0:T(8,128)(2,1)} copy(bf16[128,8192]{1,0:T(8,128)(2,1)} %get-tuple-element.6) | data formatting | bytes 4194304
  143.5 0.0 copy-done.1
  143.5 0.7 copy.13
  144.2 0.0 copy-done
  144.2 0.7 copy.14
Async XLA Ops:
  140.3 3.2 %copy-start.1 = (bf16[128,1024]{1,0:T(8,128)(2,1)S(1)}, bf16[128,1024]{1,0:T(8,128)(2,1)}, u32[]{:S(2)}) copy-start(bf16[128,1024]{1,0:T(8,128)(2,1)} %get-tuple-element.7) | copy-start | bytes 786436
  140.4 3.9 %copy-start = (bf16[128,1024]{1,0:T(8,128)(2,1)S(1)}, bf16[128,1024]{1,0:T(8,128)(2,1)}, u32[]{:S(2)}) copy-start(bf16[128,1024]{1,0:T(8,128)(2,1)} %get-tuple-element.8) | copy-start | bytes 786436

commit v2 on v1

--- a/solution.py
+++ b/solution.py
@@ -42,12 +42,15 @@
     dv_out,
     qgo,
     kv,
-    ebuf,
+    sbuf,
     bias,
-    mx,
-    zs,
-    delta,
-    dqt,
+    tops,
+    invs,
+    deltas,
+    q_t,
+    g_t,
+    probs,
+    dsc,
     acc,
     ret_out,
     ret_in,
@@ -156,18 +159,31 @@
             dkv_stage.at[g, a, theirs], dkvs[a].at[:, cols(tp * n_kv + g, HEAD_SIZE)],
             sem_dkv_s.at[a, g], sem_dkv_r.at[a, g], device_id=(ctx, other), device_id_type=MESH)
 
-    for g in range(n_kv):
+    def begin_narrow(g):
         for a in (0, 1):
             narrow_remote(a, g).start()
             narrow_local(a, g).start()
-        if g == 0:
-            wide_remote(0, 0).start()
-            wide_local(0, 0).start()
+
+    def begin_wide(a, g):
+        wide_remote(a, g).start()
+        wide_local(a, g).start()
+
+    def forward_first(g):
+        for a in (0, 1):
+            narrow_local(a, g).wait()
+            narrow_remote(a, g).wait_recv()
+            kv_y(a, g, 0).start()
+
+    begin_narrow(0)
+    begin_wide(0, 0)
+    for g in range(1, n_kv):
+        begin_narrow(g)
     for g in range(n_kv):
         for a in (0, 1, 2):
             if (a, g) != (0, 0):
-                wide_remote(a, g).start()
-                wide_local(a, g).start()
+                begin_wide(a, g)
+    forward_first(0)
+    forward_first(1)
 
     first = (ctx * SHARD).astype(F32)
     docs = len_ref.shape[1]
@@ -177,8 +193,9 @@
     starts = jnp.sum(jnp.where(c_d < r_d, jnp.broadcast_to(lens, (docs, docs)), 0.0), axis=1, keepdims=True)
     pos = lax.broadcasted_iota(jnp.int32, (docs, SHARD), 1).astype(F32) + first
     begin = jnp.max(jnp.where(starts <= pos, jnp.broadcast_to(starts, (docs, SHARD)), 0.0), axis=0, keepdims=True)
-    q_row = lax.broadcasted_iota(jnp.int32, (SHARD, SHARD), 1).astype(F32) + first
-    k_row = lax.broadcasted_iota(jnp.int32, (SHARD, SHARD), 0).astype(F32) + first
+    begin = jnp.broadcast_to(begin, (SHARD, SHARD)).T
+    q_row = lax.broadcasted_iota(jnp.int32, (SHARD, SHARD), 0).astype(F32) + first
+    k_row = lax.broadcasted_iota(jnp.int32, (SHARD, SHARD), 1).astype(F32) + first
 
     def write_bias(s, carry):
         k_pos = k_row - (s * SHARD).astype(F32)
@@ -187,18 +204,12 @@
         return carry
 
     lax.fori_loop(0, SLOTS, write_bias, 0)
-
-    for g in range(n_kv):
-        for a in (0, 1):
-            narrow_local(a, g).wait()
-            narrow_remote(a, g).wait_recv()
-            kv_y(a, g, 0).start()
+    dsc[...] = jnp.zeros_like(dsc)
 
     def forward_x(g):
         for a in (0, 1):
             kv_y(a, g, 0).wait_recv()
-        for a in (0, 1):
-            for d in (1, 2, 3):
+            for d in (1, 3, 2):
                 kv_x(a, g, d).start()
 
     def forward_y(g, d):
@@ -234,79 +245,78 @@
     def back_end(g):
         par = lax.rem(g, 2)
         ret_y(g, ROW).wait_recv()
-        total = (acc[par, 0] + ret_in[g, ROW].astype(F32)).astype(BF16)
-        dkv_stage[g] = total
         for a in (0, 1):
+            total = acc[par, 0, a] + ret_in[g, ROW, a].astype(F32)
+            dkv_stage[g, a] = total.T.astype(BF16)
             dkv_remote(a, g).start()
             dkv_local(a, g).start()
 
+    def lanes(h, size):
+        return pl.ds(pl.multiple_of(h * size, size), size)
+
     def head_cols(h):
         return slice(h * HEAD_SIZE, (h + 1) * HEAD_SIZE)
 
-    def phase_a(g, s):
-        keys = kv[0, g, s]
-        tops, sums = [], []
+    def head_rows(h):
+        return slice(h * SHARD, (h + 1) * SHARD)
+
+    def twice(t):
+        return jnp.concatenate([t, t], axis=1)
+
+    def scores_step(g, s):
+        keys_t = kv[0, g, s].T
         for h in range(width):
-            sc = dot_nt(keys, qgo[0, g, :, head_cols(h)])
+            sc = dot_nn(qgo[0, g, :, head_cols(h)], keys_t)
             sc = sc * to_exp2 + bias[s]
-            top = jnp.max(sc, axis=0, keepdims=True)
-            e = jnp.exp2(sc - top)
-            ebuf[s, h] = e
-            tops.append(top)
-            sums.append(jnp.sum(e, axis=0, keepdims=True))
-        mx[s] = jnp.concatenate(tops, axis=0)
-        zs[s] = jnp.concatenate(sums, axis=0)
-
-    def normalise(g):
-        top = mx[0]
-        for s in range(1, SLOTS):
-            top = jnp.maximum(top, mx[s])
-        total = jnp.zeros_like(top)
+            sbuf[s, h] = sc
+            tops[h] = jnp.maximum(tops[h], jnp.maximum(sc[:, :HEAD_SIZE], sc[:, HEAD_SIZE:]))
+
+    def dq_head(g, h):
+        left = jnp.concatenate([dsc[s, lanes(h, SHARD)] for s in range(SLOTS)], axis=1)
+        right = kv[0, g].reshape(SLOTS * SHARD, HEAD_SIZE)
+        dq_stage[g, :, lanes(h, HEAD_SIZE)] = (dot_nn(left, right) * inv_root).astype(BF16)
+
+    def softmax_head(g, h):
+        q_h = qgo[0, g, :, lanes(h, HEAD_SIZE)]
+        g_h = qgo[1, g, :, lanes(h, HEAD_SIZE)]
+        o_h = qgo[2, g, :, lanes(h, HEAD_SIZE)]
+        q_t[:, lanes(h, SHARD)] = q_h.T
+        g_t[:, lanes(h, SHARD)] = g_h.T
+        delta = jnp.sum(g_h.astype(F32) * o_h.astype(F32), axis=1, keepdims=True)
+        deltas[h] = jnp.broadcast_to(delta, (SHARD, HEAD_SIZE))
+        top = jnp.max(tops[h], axis=1, keepdims=True)
+        total = jnp.zeros((SHARD, HEAD_SIZE), F32)
         for s in range(SLOTS):
-            f = jnp.exp2(mx[s] - top)
-            total = total + zs[s] * f
-            mx[s] = f
-        inv = 1.0 / total
-        for s in range(SLOTS):
-            mx[s] = mx[s] * inv
-        ones = jnp.ones((8, 2 * HEAD_SIZE), BF16)
+            e = jnp.exp2(sbuf[s, h] - top)
+            sbuf[s, h] = e
+            total = total + (e[:, :HEAD_SIZE] + e[:, HEAD_SIZE:])
+        total = jnp.sum(total, axis=1, keepdims=True)
+        invs[h] = jnp.broadcast_to(1.0 / total, (SHARD, HEAD_SIZE))
+
+    def grads_step(g, s):
+        values_t = kv[1, g, s].T
         for h in range(width):
-            prod = qgo[1, g, :, head_cols(h)].astype(F32) * qgo[2, g, :, head_cols(h)].astype(F32)
-            hi = prod.astype(BF16)
-            lo = (prod - hi.astype(F32)).astype(BF16)
-            delta[h : h + 1] = dot_nt(ones, jnp.concatenate([hi, lo], axis=1))[0:1]
-        dqt[...] = jnp.zeros_like(dqt)
-
-    def phase_b(g, s):
-        keys = kv[0, g, s]
-        values = kv[1, g, s]
-        keys_t = keys.T
-        f = mx[s]
-        dk = jnp.zeros((SHARD, HEAD_SIZE), F32)
-        dv = jnp.zeros((SHARD, HEAD_SIZE), F32)
-        for h in range(width):
-            q_h = qgo[0, g, :, head_cols(h)]
             g_h = qgo[1, g, :, head_cols(h)]
-            p = ebuf[s, h] * f[h : h + 1]
-            dp = dot_nt(values, g_h)
-            ds = (p * (dp - delta[h : h + 1])).astype(BF16)
-            dv = dv + dot_nn(p.astype(BF16), g_h)
-            dk = dk + dot_nn(ds, q_h)
-            dqt[h] += dot_nn(keys_t, ds)
-        return dk * inv_root, dv
-
-    def finish_dq(g):
-        for h in range(width):
-            dq_stage[g, :, head_cols(h)] = (dqt[h].T * inv_root).astype(BF16)
+            p = sbuf[s, h] * twice(invs[h])
+            dp = dot_nn(g_h, values_t)
+            probs[head_rows(h)] = p.astype(BF16)
+            dsc[s, head_rows(h)] = (p * (dp - twice(deltas[h]))).astype(BF16)
+        dk = dot_nn(q_t[...], dsc[s]) * inv_root
+        dv = dot_nn(g_t[...], probs[...])
+        return dk, dv
+
+    def send_dq(g):
         dq_remote(g).start()
         dq_local(g).start()
 
     def head_step(g, carry):
         par = lax.rem(g, 2)
+        before = jnp.maximum(g - 1, 0)
         wide_local(0, g).wait()
         wide_remote(0, g).wait_recv()
-
-        def a_step(i, carry_a):
+        tops[...] = jnp.full(tops.shape, 2 * NEG, F32)
+
+        def scores_of(i, carry_a):
             s = lax.select(i == 0, 0, lax.select(i == 1, ROW, lax.select(i < 5, i - 1, i)))
 
             @pl.when((g == 0) & (i == 1))
@@ -317,48 +327,65 @@
             def _():
                 forward_y(g, i - 1)
 
+            @pl.when((g == 0) & (i == 5))
+            def _():
+                forward_x(1)
+                for later in range(2, n_kv):
+                    forward_first(later)
+
+            @pl.when((g > 1) & (i == 0))
+            def _():
+                back_y(g - 2)
+
             @pl.when(i >= 5)
             def _():
                 kv_y(0, g, i - ROW).wait_recv()
 
-            @pl.when((g > 0) & (i == 5))
-            def _():
-                back_x(g - 1)
-
-            phase_a(g, s)
+            scores_step(g, s)
             return carry_a
 
-        lax.fori_loop(0, SLOTS, a_step, 0)
+        lax.fori_loop(0, SLOTS, scores_of, 0)
 
         for a in (1, 2):
             wide_local(a, g).wait()
             wide_remote(a, g).wait_recv()
-        normalise(g)
-
-        def b_step(i, carry_b):
+
+        def softmax_of(h, carry_s):
+            dq_head(before, h)
+            softmax_head(g, h)
+            return carry_s
+
+        lax.fori_loop(0, width, softmax_of, 0)
+
+        @pl.when(g > 0)
+        def _():
+            send_dq(g - 1)
+
+        def grads_of(i, carry_b):
             s = lax.select(i < 3, i + 5, lax.rem(i + 3, 5))
 
+            @pl.when((g < n_kv - 1) & (i == 0))
+            def _():
+                for d in (1, 3, 2):
+                    forward_y(g + 1, d)
+
+            @pl.when((g < n_kv - 2) & (i == 4))
+            def _():
+                forward_x(g + 2)
+
+            @pl.when((g > 0) & (i == 0))
+            def _():
+                back_x(g - 1)
+
+            @pl.when((g > 1) & (i == 0))
+            def _():
+                back_end(g - 2)
+
             @pl.when(i < 3)
             def _():
                 kv_y(1, g, i + 1).wait_recv()
 
-            @pl.when((g < n_kv - 1) & (i == 0))
-            def _():
-                forward_x(g + 1)
-
-            @pl.when((g < n_kv - 1) & (i >= 3) & (i < 6))
-            def _():
-                forward_y(g + 1, i - 2)
-
-            @pl.when((g > 0) & (i == 2))
-            def _():
-                back_y(g - 1)
-
-            @pl.when((g > 0) & (i == 7))
-            def _():
-                back_end(g - 1)
-
-            dk, dv = phase_b(g, s)
+            dk, dv = grads_step(g, s)
 
             @pl.when(i < 3)
             def _():
@@ -373,14 +400,22 @@
 
             return carry_b
 
-        lax.fori_loop(0, SLOTS, b_step, 0)
-        finish_dq(g)
+        lax.fori_loop(0, SLOTS, grads_of, 0)
         return carry
 
     lax.fori_loop(0, n_kv, head_step, 0)
     last = jnp.int32(n_kv - 1)
+    back_y(last - 1)
     back_x(last)
+
+    def last_dq(h, carry):
+        dq_head(last, h)
+        return carry
+
+    lax.fori_loop(0, width, last_dq, 0)
+    send_dq(last)
     back_y(last)
+    back_end(last - 1)
     back_end(last)
 
     def drain(g, carry):
@@ -429,13 +464,16 @@
             pltpu.VMEM((2, n_kv, SLOTS, SHARD, HEAD_SIZE), BF16),
             pltpu.VMEM((SLOTS, width, SHARD, SHARD), F32),
             pltpu.VMEM((SLOTS, SHARD, SHARD), F32),
-            pltpu.VMEM((SLOTS, width, SHARD), F32),
-            pltpu.VMEM((SLOTS, width, SHARD), F32),
-            pltpu.VMEM((width, SHARD), F32),
-            pltpu.VMEM((width, HEAD_SIZE, SHARD), F32),
-            pltpu.VMEM((2, ROW + 1, 2, SHARD, HEAD_SIZE), F32),
-            pltpu.VMEM((n_kv, SLOTS, 2, SHARD, HEAD_SIZE), BF16),
-            pltpu.VMEM((n_kv, SLOTS, 2, SHARD, HEAD_SIZE), BF16),
+            pltpu.VMEM((width, SHARD, HEAD_SIZE), F32),
+            pltpu.VMEM((width, SHARD, HEAD_SIZE), F32),
+            pltpu.VMEM((width, SHARD, HEAD_SIZE), F32),
+            pltpu.VMEM((HEAD_SIZE, width * SHARD), BF16),
+            pltpu.VMEM((HEAD_SIZE, width * SHARD), BF16),
+            pltpu.VMEM((width * SHARD, SHARD), BF16),
+            pltpu.VMEM((SLOTS, width * SHARD, SHARD), BF16),
+            pltpu.VMEM((2, ROW + 1, 2, HEAD_SIZE, SHARD), F32),
+            pltpu.VMEM((n_kv, SLOTS, 2, HEAD_SIZE, SHARD), BF16),
+            pltpu.VMEM((n_kv, SLOTS, 2, HEAD_SIZE, SHARD), BF16),
             pltpu.VMEM((n_kv, SHARD, wide), BF16),
             pltpu.VMEM((n_kv, 2, SHARD, HEAD_SIZE), BF16),
             dma((3, n_kv)),
@@ -456,7 +494,7 @@
             dma((2, n_kv)),
         ],
         compiler_params=pltpu.CompilerParams(
-            collective_id=0, has_side_effects=True, vmem_limit_bytes=60 * 1024 * 1024
+            collective_id=0, has_side_effects=True, vmem_limit_bytes=62 * 1024 * 1024
         ),
         cost_estimate=pl.CostEstimate(
             flops=flops, bytes_accessed=10 * 1024 * 1024, transcendentals=flops // (10 * HEAD_SIZE)

time: 145 us -> 113 us (0.78)
  Pallas kernels: 140 us -> 108 us
    pallas_call x1, Pallas kernels: 140 us -> 108 us  [per_device(): pl.pallas_call(functools.partial(kernel, n_ctx, n_kv, width), out_shape=(...]
where the time goes in v2:
time: 113 us
  Pallas kernels  108 us (96%)
  local copies, waits for them, and re-layouts  4.56 us (4%)
    pallas_call x1, Pallas kernels, per_device(): pl.pallas_call(functools.partial(kernel, n_ctx, n_kv, width), out_shape=(...  108 us
    unnamed x7, local copies, waits for them, and re-layouts  4.56 us

profile of v2, /device:TPU:1, one launch (start us, length us, event | category | flops | bytes accessed | tf_op | source)
XLA Modules:
  0.0 113.0 jit_solution(3879660017306872699)
XLA Ops:
  0.6 107.8 %attention_backward.1 = (bf16[128,8192]{1,0:T(8,128)(2,1)}, bf16[128,1024]{1,0:T(8,128)(2,1)}, bf16[128,1024]{1,0:T(8,128)(2,1)}) custom-call(bf16[128,8192]{1,0:T(8,128)(2,1)} %q_in.1, bf16[128,1024]{1,0:T(8,128)(2,1)} %k_in.1, bf16[128,1024]{1,0:T(8,128)(2,1)} %v_in.1, bf16[128,8192]{1,0:T(8,128)(2,1)} %o_in.1, bf16[128,8192]{1,0:T(8,128)(2,1)} %g_in.1, ...), custom_call_target="tpu_custom_call" | custom-call | flops 21474836480 | bytes 10485760 | tf_op jit(solution)/shard_map/attention_backward/pallas_call | solution.py:453
  108.4 0.0 copy-start.1
  108.4 0.0 copy-start
  108.4 3.2 %copy.12 = bf16[128,8192]{1,0:T(8,128)(2,1)} copy(bf16[128,8192]{1,0:T(8,128)(2,1)} %get-tuple-element.6) | data formatting | bytes 4194304
  111.6 0.0 copy-done.1
  111.6 0.7 copy.13
  112.3 0.0 copy-done
  112.3 0.7 copy.14
Async XLA Ops:
  108.4 3.2 %copy-start.1 = (bf16[128,1024]{1,0:T(8,128)(2,1)S(1)}, bf16[128,1024]{1,0:T(8,128)(2,1)}, u32[]{:S(2)}) copy-start(bf16[128,1024]{1,0:T(8,128)(2,1)} %get-tuple-element.7) | copy-start | bytes 786436
  108.4 3.9 %copy-start = (bf16[128,1024]{1,0:T(8,128)(2,1)S(1)}, bf16[128,1024]{1,0:T(8,128)(2,1)}, u32[]{:S(2)}) copy-start(bf16[128,1024]{1,0:T(8,128)(2,1)} %get-tuple-element.8) | copy-start | bytes 786436

commit v3 on v2

--- a/solution.py
+++ b/solution.py
@@ -42,9 +42,12 @@
     dv_out,
     qgo,
     kv,
-    sbuf,
+    sbuf0,
+    sbuf1,
     bias,
-    tops,
+    tops0,
+    tops1,
+    k_t,
     invs,
     deltas,
     q_t,
@@ -90,8 +93,6 @@
     barrier = pltpu.get_barrier_semaphore()
     for peer in [(ctx, other), (up, tp), (down, tp)] + [(along(d), tp) for d in (1, 2, 3)]:
         pl.semaphore_signal(barrier, inc=1, device_id=peer, device_id_type=MESH)
-    pl.semaphore_wait(barrier, 6)
-
     def cols(head, size):
         return pl.ds(pl.multiple_of(head * size, size), size)
 
@@ -129,15 +130,15 @@
             kv.at[a, g, held], kv.at[a, g, d],
             sem_kv_s.at[a, g, d], sem_kv_r.at[a, g, d], device_id=(along(d), tp), device_id_type=MESH)
 
-    def ret_y(g, slot):
-        return pltpu.make_async_remote_copy(
-            ret_out.at[g, slot], ret_in.at[g, slot],
-            sem_ret_s.at[g, slot], sem_ret_r.at[g, slot], device_id=(down, tp), device_id_type=MESH)
-
-    def ret_x(g, d):
-        return pltpu.make_async_remote_copy(
-            ret_out.at[g, d], ret_in.at[g, d],
-            sem_ret_s.at[g, d], sem_ret_r.at[g, d], device_id=(along(ROW - d), tp), device_id_type=MESH)
+    def ret_y(a, g, slot):
+        return pltpu.make_async_remote_copy(
+            ret_out.at[g, slot, a], ret_in.at[g, slot, a],
+            sem_ret_s.at[a, g, slot], sem_ret_r.at[a, g, slot], device_id=(down, tp), device_id_type=MESH)
+
+    def ret_x(a, g, d):
+        return pltpu.make_async_remote_copy(
+            ret_out.at[g, d, a], ret_in.at[g, d, a],
+            sem_ret_s.at[a, g, d], sem_ret_r.at[a, g, d], device_id=(along(ROW - d), tp), device_id_type=MESH)
 
     def dq_local(g):
         return pltpu.make_async_copy(
@@ -159,31 +160,26 @@
             dkv_stage.at[g, a, theirs], dkvs[a].at[:, cols(tp * n_kv + g, HEAD_SIZE)],
             sem_dkv_s.at[a, g], sem_dkv_r.at[a, g], device_id=(ctx, other), device_id_type=MESH)
 
-    def begin_narrow(g):
+    def start_remote(g):
         for a in (0, 1):
             narrow_remote(a, g).start()
+
+    def forward_first(a, g):
+        narrow_local(a, g).wait()
+        narrow_remote(a, g).wait_recv()
+        kv_y(a, g, 0).start()
+        for d in (1, 3, 2):
+
+            @pl.when(x + d < ROW)
+            def _(d=d):
+                kv_x(a, g, d).start()
+
+    for g in range(n_kv):
+        for a in (0, 1):
             narrow_local(a, g).start()
-
-    def begin_wide(a, g):
-        wide_remote(a, g).start()
-        wide_local(a, g).start()
-
-    def forward_first(g):
-        for a in (0, 1):
-            narrow_local(a, g).wait()
-            narrow_remote(a, g).wait_recv()
-            kv_y(a, g, 0).start()
-
-    begin_narrow(0)
-    begin_wide(0, 0)
-    for g in range(1, n_kv):
-        begin_narrow(g)
     for g in range(n_kv):
         for a in (0, 1, 2):
-            if (a, g) != (0, 0):
-                begin_wide(a, g)
-    forward_first(0)
-    forward_first(1)
+            wide_local(a, g).start()
 
     first = (ctx * SHARD).astype(F32)
     docs = len_ref.shape[1]
@@ -204,48 +200,60 @@
         return carry
 
     lax.fori_loop(0, SLOTS, write_bias, 0)
-    dsc[...] = jnp.zeros_like(dsc)
-
-    def forward_x(g):
+
+    pl.semaphore_wait(barrier, 6)
+    start_remote(0)
+    wide_remote(0, 0).start()
+    start_remote(1)
+    forward_first(0, 0)
+    forward_first(1, 0)
+    for g in range(2, n_kv):
+        start_remote(g)
+    for g in range(n_kv):
+        for a in (0, 1, 2):
+            if (a, g) != (0, 0):
+                wide_remote(a, g).start()
+    forward_first(0, 1)
+    forward_first(1, 1)
+
+    def forward_x(a, g):
+        kv_y(a, g, 0).wait_recv()
+        for d in (1, 3, 2):
+
+            @pl.when(x + d >= ROW)
+            def _(d=d):
+                kv_x(a, g, d).start()
+
+    def forward_y(a, g, d):
+        kv_x(a, g, d).wait_recv()
+        kv_y(a, g, d).start()
+
+    def back_x(g, d):
+        par = lax.rem(g, 2)
         for a in (0, 1):
-            kv_y(a, g, 0).wait_recv()
-            for d in (1, 3, 2):
-                kv_x(a, g, d).start()
-
-    def forward_y(g, d):
-        for a in (0, 1):
-            kv_x(a, g, d).wait_recv()
-            kv_y(a, g, d).start()
-
-    def back_x(g):
-        par = lax.rem(g, 2)
-
-        def one(d, carry):
-            ret_y(g, ROW + d).wait_recv()
-            ret_out[g, d] = (acc[par, d] + ret_in[g, ROW + d].astype(F32)).astype(BF16)
-            ret_x(g, d).start()
-            return carry
-
-        lax.fori_loop(1, ROW, one, 0)
+            ret_y(a, g, ROW + d).wait_recv()
+            ret_out[g, d, a] = (acc[par, d, a] + ret_in[g, ROW + d, a].astype(F32)).astype(BF16)
+            ret_x(a, g, d).start()
 
     def back_y(g):
         par = lax.rem(g, 2)
-        far = acc[par, ROW]
-        near = acc[par, 0]
-        for d in (1, 2, 3):
-            ret_x(g, d).wait_recv()
-            part = ret_in[g, d].astype(F32)
-            crosses = ((x + d) // ROW).astype(F32)
-            far = far + part * crosses
-            near = near + part * (1.0 - crosses)
-        ret_out[g, ROW] = far.astype(BF16)
-        ret_y(g, ROW).start()
-        acc[par, 0] = near
+        for a in (0, 1):
+            far = acc[par, ROW, a]
+            near = acc[par, 0, a]
+            for d in (1, 2, 3):
+                ret_x(a, g, d).wait_recv()
+                part = ret_in[g, d, a].astype(F32)
+                crosses = ((x + d) // ROW).astype(F32)
+                far = far + part * crosses
+                near = near + part * (1.0 - crosses)
+            ret_out[g, ROW, a] = far.astype(BF16)
+            ret_y(a, g, ROW).start()
+            acc[par, 0, a] = near
 
     def back_end(g):
         par = lax.rem(g, 2)
-        ret_y(g, ROW).wait_recv()
         for a in (0, 1):
+            ret_y(a, g, ROW).wait_recv()
             total = acc[par, 0, a] + ret_in[g, ROW, a].astype(F32)
             dkv_stage[g, a] = total.T.astype(BF16)
             dkv_remote(a, g).start()
@@ -263,41 +271,65 @@
     def twice(t):
         return jnp.concatenate([t, t], axis=1)
 
+    sbufs = (sbuf0, sbuf1)
+    topss = (tops0, tops1)
+
+    def halves_max(sc):
+        return jnp.maximum(sc[:, :HEAD_SIZE], sc[:, HEAD_SIZE:])
+
     def scores_step(g, s):
         keys_t = kv[0, g, s].T
         for h in range(width):
+            tops = topss[h % 2]
             sc = dot_nn(qgo[0, g, :, head_cols(h)], keys_t)
             sc = sc * to_exp2 + bias[s]
-            sbuf[s, h] = sc
-            tops[h] = jnp.maximum(tops[h], jnp.maximum(sc[:, :HEAD_SIZE], sc[:, HEAD_SIZE:]))
+            sbufs[h % 2][s, h // 2] = sc
+            tops[h // 2] = jnp.maximum(tops[h // 2], halves_max(sc))
 
     def dq_head(g, h):
         left = jnp.concatenate([dsc[s, lanes(h, SHARD)] for s in range(SLOTS)], axis=1)
         right = kv[0, g].reshape(SLOTS * SHARD, HEAD_SIZE)
         dq_stage[g, :, lanes(h, HEAD_SIZE)] = (dot_nn(left, right) * inv_root).astype(BF16)
 
-    def softmax_head(g, h):
-        q_h = qgo[0, g, :, lanes(h, HEAD_SIZE)]
-        g_h = qgo[1, g, :, lanes(h, HEAD_SIZE)]
-        o_h = qgo[2, g, :, lanes(h, HEAD_SIZE)]
-        q_t[:, lanes(h, SHARD)] = q_h.T
-        g_t[:, lanes(h, SHARD)] = g_h.T
-        delta = jnp.sum(g_h.astype(F32) * o_h.astype(F32), axis=1, keepdims=True)
-        deltas[h] = jnp.broadcast_to(delta, (SHARD, HEAD_SIZE))
-        top = jnp.max(tops[h], axis=1, keepdims=True)
-        total = jnp.zeros((SHARD, HEAD_SIZE), F32)
+    def heads_step(g, new, old, before):
+        if new is not None:
+            h = 2 * new[0] + new[1]
+            if before is not None:
+                dq_head(before, h)
+            q_new = qgo[0, g, :, lanes(h, HEAD_SIZE)]
+            reach = None
+        if old is not None:
+            h = 2 * old[0] + old[1]
+            sbuf = sbufs[old[1]]
+            top = jnp.max(topss[old[1]][old[0]], axis=1, keepdims=True)
+            total = jnp.zeros((SHARD, HEAD_SIZE), F32)
         for s in range(SLOTS):
-            e = jnp.exp2(sbuf[s, h] - top)
-            sbuf[s, h] = e
-            total = total + (e[:, :HEAD_SIZE] + e[:, HEAD_SIZE:])
-        total = jnp.sum(total, axis=1, keepdims=True)
-        invs[h] = jnp.broadcast_to(1.0 / total, (SHARD, HEAD_SIZE))
+            if old is not None:
+                e = jnp.exp2(sbuf[s, old[0]] - top)
+                sbuf[s, old[0]] = e
+                total = total + (e[:, :HEAD_SIZE] + e[:, HEAD_SIZE:])
+            if new is not None:
+                sc = dot_nn(q_new, k_t[s]) * to_exp2 + bias[s]
+                sbufs[new[1]][s, new[0]] = sc
+                reach = halves_max(sc) if reach is None else jnp.maximum(reach, halves_max(sc))
+        if new is not None:
+            topss[new[1]][new[0]] = reach
+        if old is not None:
+            q_h = qgo[0, g, :, lanes(h, HEAD_SIZE)]
+            g_h = qgo[1, g, :, lanes(h, HEAD_SIZE)]
+            o_h = qgo[2, g, :, lanes(h, HEAD_SIZE)]
+            q_t[:, lanes(h, SHARD)] = q_h.T
+            g_t[:, lanes(h, SHARD)] = g_h.T
+            delta = jnp.sum(g_h.astype(F32) * o_h.astype(F32), axis=1, keepdims=True)
+            deltas[h] = jnp.broadcast_to(delta, (SHARD, HEAD_SIZE))
+            total = jnp.sum(total, axis=1, keepdims=True)
+            invs[h] = jnp.broadcast_to(1.0 / total, (SHARD, HEAD_SIZE))
 
     def grads_step(g, s):
         values_t = kv[1, g, s].T
         for h in range(width):
             g_h = qgo[1, g, :, head_cols(h)]
-            p = sbuf[s, h] * twice(invs[h])
+            p = sbufs[h % 2][s, h // 2] * twice(invs[h])
             dp = dot_nn(g_h, values_t)
             probs[head_rows(h)] = p.astype(BF16)
             dsc[s, head_rows(h)] = (p * (dp - twice(deltas[h]))).astype(BF16)
@@ -314,51 +346,82 @@
         before = jnp.maximum(g - 1, 0)
         wide_local(0, g).wait()
         wide_remote(0, g).wait_recv()
-        tops[...] = jnp.full(tops.shape, 2 * NEG, F32)
-
-        def scores_of(i, carry_a):
-            s = lax.select(i == 0, 0, lax.select(i == 1, ROW, lax.select(i < 5, i - 1, i)))
-
-            @pl.when((g == 0) & (i == 1))
-            def _():
-                forward_x(g)
-
-            @pl.when((g == 0) & (i >= 2) & (i < 5))
-            def _():
-                forward_y(g, i - 1)
-
-            @pl.when((g == 0) & (i == 5))
-            def _():
-                forward_x(1)
-                for later in range(2, n_kv):
-                    forward_first(later)
-
-            @pl.when((g > 1) & (i == 0))
-            def _():
-                back_y(g - 2)
-
-            @pl.when(i >= 5)
-            def _():
-                kv_y(0, g, i - ROW).wait_recv()
-
-            scores_step(g, s)
-            return carry_a
-
-        lax.fori_loop(0, SLOTS, scores_of, 0)
-
-        for a in (1, 2):
-            wide_local(a, g).wait()
-            wide_remote(a, g).wait_recv()
-
-        def softmax_of(h, carry_s):
-            dq_head(before, h)
-            softmax_head(g, h)
-            return carry_s
-
-        lax.fori_loop(0, width, softmax_of, 0)
+
+        @pl.when(g > 1)
+        def _():
+            back_y(g - 2)
+
+        @pl.when(g == 0)
+        def _():
+            tops0[...] = jnp.full(tops0.shape, 2 * NEG, F32)
+            tops1[...] = jnp.full(tops1.shape, 2 * NEG, F32)
+
+            def scores_of(i, carry_a):
+                d = lax.select(i < 5, lax.select(i == 3, 3, lax.select(i == 4, 2, 1)),
+                               lax.select(i == 6, 3, lax.select(i == 7, 2, 1)))
+                s = lax.select(i == 0, 0, lax.select(i == 1, ROW, lax.select(i < 5, d, ROW + d)))
+
+                @pl.when(i == 1)
+                def _():
+                    forward_x(0, g)
+
+                @pl.when(i == 2)
+                def _():
+                    forward_x(1, g)
+
+                @pl.when((i >= 2) & (i < 5))
+                def _():
+                    forward_y(0, g, d)
+
+                @pl.when(i == 5)
+                def _():
+                    for e in (1, 3, 2):
+                        forward_y(1, g, e)
+                    for later in range(2, n_kv):
+                        for a in (0, 1):
+                            forward_first(a, later)
+                    for a in (0, 1):
+                        forward_x(a, 1)
+
+                @pl.when(i >= 5)
+                def _():
+                    kv_y(0, g, d).wait_recv()
+
+                scores_step(g, s)
+                return carry_a
+
+            lax.fori_loop(0, SLOTS, scores_of, 0)
+            for a in (1, 2):
+                wide_local(a, g).wait()
+                wide_remote(a, g).wait_recv()
+
+            def softmax_of(j, carry_s):
+                heads_step(g, None, (j, 0), None)
+                heads_step(g, None, (j, 1), None)
+                return carry_s
+
+            lax.fori_loop(0, width // 2, softmax_of, 0)
 
         @pl.when(g > 0)
         def _():
+            for d in (1, 3, 2):
+                kv_y(0, g, d).wait_recv()
+            for a in (1, 2):
+                wide_local(a, g).wait()
+                wide_remote(a, g).wait_recv()
+            for s in range(SLOTS):
+                k_t[s] = kv[0, g, s].T
+            heads_step(g, (0, 0), None, before)
+
+            def heads_of(j, carry_s):
+                heads_step(g, (j, 1), (j, 0), before)
+                heads_step(g, (j + 1, 0), (j, 1), before)
+                return carry_s
+
+            lax.fori_loop(0, width // 2 - 1, heads_of, 0)
+            tail = width // 2 - 1
+            heads_step(g, (tail, 1), (tail, 0), before)
+            heads_step(g, None, (tail, 1), None)
             send_dq(g - 1)
 
         def grads_of(i, carry_b):
@@ -366,16 +429,19 @@
 
             @pl.when((g < n_kv - 1) & (i == 0))
             def _():
-                for d in (1, 3, 2):
-                    forward_y(g + 1, d)
+                for a in (0, 1):
+                    for d in (1, 3, 2):
+                        forward_y(a, g + 1, d)
 
             @pl.when((g < n_kv - 2) & (i == 4))
             def _():
-                forward_x(g + 2)
+                for a in (0, 1):
+                    forward_x(a, g + 2)
 
             @pl.when((g > 0) & (i == 0))
             def _():
-                back_x(g - 1)
+                for d in (1, 2, 3):
+                    back_x(g - 1, d)
 
             @pl.when((g > 1) & (i == 0))
             def _():
@@ -390,8 +456,9 @@
             @pl.when(i < 3)
             def _():
                 ret_out[g, s, 0] = dk.astype(BF16)
+                ret_y(0, g, s).start()
                 ret_out[g, s, 1] = dv.astype(BF16)
-                ret_y(g, s).start()
+                ret_y(1, g, s).start()
 
             @pl.when(i >= 3)
             def _():
@@ -405,20 +472,12 @@
 
     lax.fori_loop(0, n_kv, head_step, 0)
     last = jnp.int32(n_kv - 1)
-    back_y(last - 1)
-    back_x(last)
 
     def last_dq(h, carry):
         dq_head(last, h)
         return carry
 
-    lax.fori_loop(0, width, last_dq, 0)
-    send_dq(last)
-    back_y(last)
-    back_end(last - 1)
-    back_end(last)
-
-    def drain(g, carry):
+    def drain_early(g, carry):
         for a in (0, 1, 2):
             wide_remote(a, g).wait_send()
         for a in (0, 1):
@@ -427,12 +486,28 @@
                 kv_y(a, g, d).wait_send()
             for d in (1, 2, 3):
                 kv_x(a, g, d).wait_send()
+        return carry
+
+    back_x(last, 1)
+    lax.fori_loop(0, width // 2, last_dq, 0)
+    back_y(last - 1)
+    back_x(last, 2)
+    lax.fori_loop(width // 2, width, last_dq, 0)
+    back_x(last, 3)
+    send_dq(last)
+    back_end(last - 1)
+    lax.fori_loop(0, n_kv, drain_early, 0)
+    back_y(last)
+    back_end(last)
+
+    def drain(g, carry):
+        for a in (0, 1):
+            for s in range(ROW, SLOTS):
+                ret_y(a, g, s).wait_send()
+            for d in (1, 2, 3):
+                ret_x(a, g, d).wait_send()
             dkv_local(a, g).wait()
             dkv_remote(a, g).wait()
-        for s in range(ROW, SLOTS):
-            ret_y(g, s).wait_send()
-        for d in (1, 2, 3):
-            ret_x(g, d).wait_send()
         dq_local(g).wait()
         dq_remote(g).wait()
         return carry
@@ -450,7 +525,7 @@
     wide = width * HEAD_SIZE
     dma = pltpu.SemaphoreType.DMA
     flops = 5 * 2 * SHARD * SLOTS * SHARD * HEAD_SIZE * n_kv * width
-    return pl.pallas_call(
+    raw = pl.pallas_call(
         functools.partial(kernel, n_ctx, n_kv, width),
         out_shape=(
             jax.ShapeDtypeStruct(queries.shape, BF16),
@@ -462,9 +537,12 @@
         scratch_shapes=[
             pltpu.VMEM((3, n_kv, SHARD, wide), BF16),
             pltpu.VMEM((2, n_kv, SLOTS, SHARD, HEAD_SIZE), BF16),
-            pltpu.VMEM((SLOTS, width, SHARD, SHARD), F32),
+            pltpu.VMEM((SLOTS, width // 2, SHARD, SHARD), F32),
+            pltpu.VMEM((SLOTS, width // 2, SHARD, SHARD), F32),
             pltpu.VMEM((SLOTS, SHARD, SHARD), F32),
-            pltpu.VMEM((width, SHARD, HEAD_SIZE), F32),
+            pltpu.VMEM((width // 2, SHARD, HEAD_SIZE), F32),
+            pltpu.VMEM((width // 2, SHARD, HEAD_SIZE), F32),
+            pltpu.VMEM((SLOTS, HEAD_SIZE, SHARD), BF16),
             pltpu.VMEM((width, SHARD, HEAD_SIZE), F32),
             pltpu.VMEM((width, SHARD, HEAD_SIZE), F32),
             pltpu.VMEM((HEAD_SIZE, width * SHARD), BF16),
@@ -484,8 +562,8 @@
             dma((2, n_kv)),
             dma((2, n_kv, SLOTS)),
             dma((2, n_kv, SLOTS)),
-            dma((n_kv, SLOTS)),
-            dma((n_kv, SLOTS)),
+            dma((2, n_kv, SLOTS)),
+            dma((2, n_kv, SLOTS)),
             dma((n_kv,)),
             dma((n_kv,)),
             dma((n_kv,)),
@@ -508,6 +586,39 @@
         output_gradient,
         lengths.reshape(1, lengths.shape[0]),
     )
+    return hand_over(*raw)
+
+
+def hand_over_kernel(parts, dq_in, dk_in, dv_in, dq_out, dk_out, dv_out, dq_mid, dk_mid, dv_mid, sem_in, sem_out):
+    rows = HALF // parts
+    pieces = [(dk_in, dk_mid, dk_out), (dv_in, dv_mid, dv_out)]
+    for i in range(parts):
+        part = pl.ds(i * rows, rows)
+        pieces.append((dq_in.at[part], dq_mid.at[part], dq_out.at[part]))
+    loads = [pltpu.make_async_copy(a, b, sem_in.at[i]) for i, (a, b, _) in enumerate(pieces)]
+    stores = [pltpu.make_async_copy(b, c, sem_out.at[i]) for i, (_, b, c) in enumerate(pieces)]
+    for load in loads:
+        load.start()
+    for load, store in zip(loads, stores):
+        load.wait()
+        store.start()
+    for store in stores:
+        store.wait()
+
+
+def hand_over(dq, dk, dv):
+    parts = 8
+    any_spec = pl.BlockSpec(memory_space=pl.ANY)
+    arrays = (dq, dk, dv)
+    return pl.pallas_call(
+        functools.partial(hand_over_kernel, parts),
+        out_shape=tuple(jax.ShapeDtypeStruct(t.shape, t.dtype) for t in arrays),
+        in_specs=[any_spec] * 3,
+        out_specs=(any_spec,) * 3,
+        scratch_shapes=[pltpu.VMEM(t.shape, t.dtype) for t in arrays]
+        + [pltpu.SemaphoreType.DMA((parts + 2,)), pltpu.SemaphoreType.DMA((parts + 2,))],
+        name="hand_over",
+    )(*arrays)
 
 
 def solution(mesh):

time: 113 us -> 105 us (0.929)
  local copies, waits for them, and re-layouts: 4.56 us -> 0 us
  Pallas kernels: 108 us -> 104 us
    pallas_call x1, Pallas kernels: 108 us -> 102 us  [per_device(): pl.pallas_call(functools.partial(kernel, n_ctx, n_kv, width), out_shape=(...]
    unnamed x7 -> x0, local copies, waits for them, and re-layouts: 4.56 us -> none
    pallas_call x0 -> x1, Pallas kernels: none -> 2.6 us  [hand_over(): pl.pallas_call(functools.partial(hand_over_kernel, parts), out_shape=tupl...]
where the time goes in v3:
time: 105 us
  Pallas kernels  104 us (99%)
    pallas_call x1, Pallas kernels, per_device(): pl.pallas_call(functools.partial(kernel, n_ctx, n_kv, width), out_shape=(...  102 us
    pallas_call x1, Pallas kernels, hand_over(): pl.pallas_call(functools.partial(hand_over_kernel, parts), out_shape=tupl...  2.6 us

profile of v3, /device:TPU:1, one launch (start us, length us, event | category | flops | bytes accessed | tf_op | source)
XLA Modules:
  0.0 105.0 jit_solution(5056673554527389976)
XLA Ops:
  0.6 101.7 %attention_backward.1 = (bf16[128,8192]{1,0:T(8,128)(2,1)}, bf16[128,1024]{1,0:T(8,128)(2,1)}, bf16[128,1024]{1,0:T(8,128)(2,1)}) custom-call(bf16[128,8192]{1,0:T(8,128)(2,1)} %q_in.1, bf16[128,1024]{1,0:T(8,128)(2,1)} %k_in.1, bf16[128,1024]{1,0:T(8,128)(2,1)} %v_in.1, bf16[128,8192]{1,0:T(8,128)(2,1)} %o_in.1, bf16[128,8192]{1,0:T(8,128)(2,1)} %g_in.1, ...), custom_call_target="tpu_custom_call" | custom-call | flops 21474836480 | bytes 10485760 | tf_op jit(solution)/shard_map/attention_backward/pallas_call | solution.py:528
  102.4 2.6 %hand_over.1 = (bf16[128,8192]{1,0:T(8,128)(2,1)}, bf16[128,1024]{1,0:T(8,128)(2,1)}, bf16[128,1024]{1,0:T(8,128)(2,1)}) custom-call(bf16[128,8192]{1,0:T(8,128)(2,1)} %get-tuple-element.6.dq_in, bf16[128,1024]{1,0:T(8,128)(2,1)} %get-tuple-element.7.dk_in, bf16[128,1024]{1,0:T(8,128)(2,1)} %get-tuple-element.8.dv_in), custom_call_target="tpu_custom_call" | custom-call | tf_op jit(solution)/shard_map/hand_over/pallas_call | solution.py:613

commit v4 on v3

--- a/solution.py
+++ b/solution.py
@@ -168,18 +168,37 @@
         narrow_local(a, g).wait()
         narrow_remote(a, g).wait_recv()
         kv_y(a, g, 0).start()
-        for d in (1, 3, 2):
-
-            @pl.when(x + d < ROW)
-            def _(d=d):
-                kv_x(a, g, d).start()
-
-    for g in range(n_kv):
+
+    for a in (0, 1):
+        narrow_local(a, 0).start()
+    wide_local(0, 0).start()
+
+    pl.semaphore_wait(barrier, 6)
+    start_remote(0)
+    wide_remote(0, 0).start()
+    start_remote(1)
+    forward_first(0, 0)
+    for d in (1, 3, 2):
+
+        @pl.when(x + d < ROW)
+        def _(d=d):
+            kv_x(0, 0, d).start()
+
+    forward_first(1, 0)
+    for g in range(1, n_kv):
         for a in (0, 1):
             narrow_local(a, g).start()
+        if g > 1:
+            start_remote(g)
+    for g in range(1, n_kv - 1):
+        for a in (0, 1):
+            forward_first(a, g)
+
     for g in range(n_kv):
         for a in (0, 1, 2):
-            wide_local(a, g).start()
+            if (a, g) != (0, 0):
+                wide_remote(a, g).start()
+                wide_local(a, g).start()
 
     first = (ctx * SHARD).astype(F32)
     docs = len_ref.shape[1]
@@ -201,28 +220,10 @@
 
     lax.fori_loop(0, SLOTS, write_bias, 0)
 
-    pl.semaphore_wait(barrier, 6)
-    start_remote(0)
-    wide_remote(0, 0).start()
-    start_remote(1)
-    forward_first(0, 0)
-    forward_first(1, 0)
-    for g in range(2, n_kv):
-        start_remote(g)
-    for g in range(n_kv):
-        for a in (0, 1, 2):
-            if (a, g) != (0, 0):
-                wide_remote(a, g).start()
-    forward_first(0, 1)
-    forward_first(1, 1)
-
     def forward_x(a, g):
         kv_y(a, g, 0).wait_recv()
         for d in (1, 3, 2):
-
-            @pl.when(x + d >= ROW)
-            def _(d=d):
-                kv_x(a, g, d).start()
+            kv_x(a, g, d).start()
 
     def forward_y(a, g, d):
         kv_x(a, g, d).wait_recv()
@@ -290,6 +291,43 @@
         left = jnp.concatenate([dsc[s, lanes(h, SHARD)] for s in range(SLOTS)], axis=1)
         right = kv[0, g].reshape(SLOTS * SHARD, HEAD_SIZE)
         dq_stage[g, :, lanes(h, HEAD_SIZE)] = (dot_nn(left, right) * inv_root).astype(BF16)
+
+    def exponentials(sbuf, hb, top, slots):
+        total = jnp.zeros((SHARD, HEAD_SIZE), F32)
+        for s in slots:
+            e = jnp.exp2(sbuf[s, hb] - top)
+            sbuf[s, hb] = e
+            total = total + (e[:, :HEAD_SIZE] + e[:, HEAD_SIZE:])
+        return total
+
+    def turn_and_delta(g, h):
+        q_h = qgo[0, g, :, lanes(h, HEAD_SIZE)]
+        g_h = qgo[1, g, :, lanes(h, HEAD_SIZE)]
+        o_h = qgo[2, g, :, lanes(h, HEAD_SIZE)]
+        q_t[:, lanes(h, SHARD)] = q_h.T
+        g_t[:, lanes(h, SHARD)] = g_h.T
+        delta = jnp.sum(g_h.astype(F32) * o_h.astype(F32), axis=1, keepdims=True)
+        deltas[h] = jnp.broadcast_to(delta, (SHARD, HEAD_SIZE))
+
+    def near_softmax(j, carry):
+        for par in (0, 1):
+            h = 2 * j + par
+            top = jnp.max(topss[par][j], axis=1, keepdims=True)
+            invs[0, h] = jnp.broadcast_to(top, (SHARD, HEAD_SIZE))
+            deltas[h] = exponentials(sbufs[par], j, top, range(ROW + 1))
+        return carry
+
+    def far_softmax(j, carry):
+        for par in (0, 1):
+            h = 2 * j + par
+            top = jnp.max(topss[par][j], axis=1, keepdims=True)
+            shrink = jnp.exp2(invs[0, h] - top)
+            total = deltas[h] * shrink + exponentials(sbufs[par], j, top, range(ROW + 1, SLOTS))
+            inv = jnp.broadcast_to(1.0 / jnp.sum(total, axis=1, keepdims=True), (SHARD, HEAD_SIZE))
+            invs[1, h] = inv
+            invs[0, h] = inv * shrink
+            turn_and_delta(0, h)
+        return carry
 
     def heads_step(g, new, old, before):
         if new is not None:
@@ -315,21 +353,17 @@
         if new is not None:
             topss[new[1]][new[0]] = reach
         if old is not None:
-            q_h = qgo[0, g, :, lanes(h, HEAD_SIZE)]
-            g_h = qgo[1, g, :, lanes(h, HEAD_SIZE)]
-            o_h = qgo[2, g, :, lanes(h, HEAD_SIZE)]
-            q_t[:, lanes(h, SHARD)] = q_h.T
-            g_t[:, lanes(h, SHARD)] = g_h.T
-            delta = jnp.sum(g_h.astype(F32) * o_h.astype(F32), axis=1, keepdims=True)
-            deltas[h] = jnp.broadcast_to(delta, (SHARD, HEAD_SIZE))
-            total = jnp.sum(total, axis=1, keepdims=True)
-            invs[h] = jnp.broadcast_to(1.0 / total, (SHARD, HEAD_SIZE))
+            turn_and_delta(g, h)
+            inv = jnp.broadcast_to(1.0 / jnp.sum(total, axis=1, keepdims=True), (SHARD, HEAD_SIZE))
+            invs[1, h] = inv
+            invs[0, h] = inv
 
     def grads_step(g, s):
         values_t = kv[1, g, s].T
+        far = lax.select(s > ROW, 1, 0)
         for h in range(width):
             g_h = qgo[1, g, :, head_cols(h)]
-            p = sbufs[h % 2][s, h // 2] * twice(invs[h])
+            p = sbufs[h % 2][s, h // 2] * twice(invs[far, h])
             dp = dot_nn(g_h, values_t)
             probs[head_rows(h)] = p.astype(BF16)
             dsc[s, head_rows(h)] = (p * (dp - twice(deltas[h]))).astype(BF16)
@@ -363,7 +397,12 @@
 
                 @pl.when(i == 1)
                 def _():
-                    forward_x(0, g)
+                    kv_y(0, g, 0).wait_recv()
+                    for e in (1, 3, 2):
+
+                        @pl.when(x + e >= ROW)
+                        def _(e=e):
+                            kv_x(0, g, e).start()
 
                 @pl.when(i == 2)
                 def _():
@@ -375,13 +414,13 @@
 
                 @pl.when(i == 5)
                 def _():
+                    for a in (0, 1):
+                        forward_x(a, 1)
+                    lax.fori_loop(0, width // 2, near_softmax, 0)
                     for e in (1, 3, 2):
                         forward_y(1, g, e)
-                    for later in range(2, n_kv):
-                        for a in (0, 1):
-                            forward_first(a, later)
                     for a in (0, 1):
-                        forward_x(a, 1)
+                        forward_first(a, n_kv - 1)
 
                 @pl.when(i >= 5)
                 def _():
@@ -395,12 +434,7 @@
                 wide_local(a, g).wait()
                 wide_remote(a, g).wait_recv()
 
-            def softmax_of(j, carry_s):
-                heads_step(g, None, (j, 0), None)
-                heads_step(g, None, (j, 1), None)
-                return carry_s
-
-            lax.fori_loop(0, width // 2, softmax_of, 0)
+            lax.fori_loop(0, width // 2, far_softmax, 0)
 
         @pl.when(g > 0)
         def _():
@@ -489,6 +523,18 @@
         return carry
 
     back_x(last, 1)
+    def drain(g, carry):
+        for a in (0, 1):
+            for s in range(ROW, SLOTS):
+                ret_y(a, g, s).wait_send()
+            for d in (1, 2, 3):
+                ret_x(a, g, d).wait_send()
+            dkv_local(a, g).wait()
+            dkv_remote(a, g).wait()
+        dq_local(g).wait()
+        dq_remote(g).wait()
+        return carry
+
     lax.fori_loop(0, width // 2, last_dq, 0)
     back_y(last - 1)
     back_x(last, 2)
@@ -498,21 +544,10 @@
     back_end(last - 1)
     lax.fori_loop(0, n_kv, drain_early, 0)
     back_y(last)
+    lax.fori_loop(0, n_kv - 1, drain, 0)
     back_end(last)
 
-    def drain(g, carry):
-        for a in (0, 1):
-            for s in range(ROW, SLOTS):
-                ret_y(a, g, s).wait_send()
-            for d in (1, 2, 3):
-                ret_x(a, g, d).wait_send()
-            dkv_local(a, g).wait()
-            dkv_remote(a, g).wait()
-        dq_local(g).wait()
-        dq_remote(g).wait()
-        return carry
-
-    lax.fori_loop(0, n_kv, drain, 0)
+    drain(last, 0)
 
 
 def per_device(queries, key_matrix, value_matrix, attention_output, output_gradient, lengths):
@@ -543,7 +578,7 @@
             pltpu.VMEM((width // 2, SHARD, HEAD_SIZE), F32),
             pltpu.VMEM((width // 2, SHARD, HEAD_SIZE), F32),
             pltpu.VMEM((SLOTS, HEAD_SIZE, SHARD), BF16),
-            pltpu.VMEM((width, SHARD, HEAD_SIZE), F32),
+            pltpu.VMEM((2, width, SHARD, HEAD_SIZE), F32),
             pltpu.VMEM((width, SHARD, HEAD_SIZE), F32),
             pltpu.VMEM((HEAD_SIZE, width * SHARD), BF16),
             pltpu.VMEM((HEAD_SIZE, width * SHARD), BF16),

time: 105 us -> 104 us (level)
    pallas_call x1, Pallas kernels: 102 us -> 100 us  [per_device(): pl.pallas_call(functools.partial(kernel, n_ctx, n_kv, width), out_shape=(...]
where the time goes in v4:
time: 104 us; the launch traced here: 103 us
  Pallas kernels  103 us (99%)
    pallas_call x1, Pallas kernels, per_device(): pl.pallas_call(functools.partial(kernel, n_ctx, n_kv, width), out_shape=(...  100 us
    pallas_call x1, Pallas kernels, hand_over(): pl.pallas_call(functools.partial(hand_over_kernel, parts), out_shape=tupl...  2.6 us

profile of v4, /device:TPU:1, one launch (start us, length us, event | category | flops | bytes accessed | tf_op | source)
XLA Modules:
  0.0 103.3 jit_solution(12675285858760864202)
XLA Ops:
  0.6 100.0 %attention_backward.1 = (bf16[128,8192]{1,0:T(8,128)(2,1)}, bf16[128,1024]{1,0:T(8,128)(2,1)}, bf16[128,1024]{1,0:T(8,128)(2,1)}) custom-call(bf16[128,8192]{1,0:T(8,128)(2,1)} %q_in.1, bf16[128,1024]{1,0:T(8,128)(2,1)} %k_in.1, bf16[128,1024]{1,0:T(8,128)(2,1)} %v_in.1, bf16[128,8192]{1,0:T(8,128)(2,1)} %o_in.1, bf16[128,8192]{1,0:T(8,128)(2,1)} %g_in.1, ...), custom_call_target="tpu_custom_call" | custom-call | flops 21474836480 | bytes 10485760 | tf_op jit(solution)/shard_map/attention_backward/pallas_call | solution.py:563
  100.7 2.6 %hand_over.1 = (bf16[128,8192]{1,0:T(8,128)(2,1)}, bf16[128,1024]{1,0:T(8,128)(2,1)}, bf16[128,1024]{1,0:T(8,128)(2,1)}) custom-call(bf16[128,8192]{1,0:T(8,128)(2,1)} %get-tuple-element.6.dq_in, bf16[128,1024]{1,0:T(8,128)(2,1)} %get-tuple-element.7.dk_in, bf16[128,1024]{1,0:T(8,128)(2,1)} %get-tuple-element.8.dv_in), custom_call_target="tpu_custom_call" | custom-call | tf_op jit(solution)/shard_map/hand_over/pallas_call | solution.py:648

commit v5 on v4

--- a/solution.py
+++ b/solution.py
@@ -132,21 +132,21 @@
 
     def ret_y(a, g, slot):
         return pltpu.make_async_remote_copy(
-            ret_out.at[g, slot, a], ret_in.at[g, slot, a],
+            ret_out.at[g, slot - 1, a], ret_in.at[g, slot - 1, a],
             sem_ret_s.at[a, g, slot], sem_ret_r.at[a, g, slot], device_id=(down, tp), device_id_type=MESH)
 
     def ret_x(a, g, d):
         return pltpu.make_async_remote_copy(
-            ret_out.at[g, d, a], ret_in.at[g, d, a],
+            ret_out.at[g, d - 1, a], ret_in.at[g, d - 1, a],
             sem_ret_s.at[a, g, d], sem_ret_r.at[a, g, d], device_id=(along(ROW - d), tp), device_id_type=MESH)
 
     def dq_local(g):
         return pltpu.make_async_copy(
-            dq_stage.at[g, mine], dq_out.at[:, cols(tp * n_kv + g, wide)], sem_dq_l.at[g])
+            dq_stage.at[lax.rem(g, 2), mine], dq_out.at[:, cols(tp * n_kv + g, wide)], sem_dq_l.at[g])
 
     def dq_remote(g):
         return pltpu.make_async_remote_copy(
-            dq_stage.at[g, theirs], dq_out.at[:, cols(tp * n_kv + g, wide)],
+            dq_stage.at[lax.rem(g, 2), theirs], dq_out.at[:, cols(tp * n_kv + g, wide)],
             sem_dq_s.at[g], sem_dq_r.at[g], device_id=(ctx, other), device_id_type=MESH)
 
     dkvs = (dk_out, dv_out)
@@ -233,7 +233,7 @@
         par = lax.rem(g, 2)
         for a in (0, 1):
             ret_y(a, g, ROW + d).wait_recv()
-            ret_out[g, d, a] = (acc[par, d, a] + ret_in[g, ROW + d, a].astype(F32)).astype(BF16)
+            ret_out[g, d - 1, a] = (acc[par, d, a] + ret_in[g, ROW + d - 1, a].astype(F32)).astype(BF16)
             ret_x(a, g, d).start()
 
     def back_y(g):
@@ -243,11 +243,11 @@
             near = acc[par, 0, a]
             for d in (1, 2, 3):
                 ret_x(a, g, d).wait_recv()
-                part = ret_in[g, d, a].astype(F32)
+                part = ret_in[g, d - 1, a].astype(F32)
                 crosses = ((x + d) // ROW).astype(F32)
                 far = far + part * crosses
                 near = near + part * (1.0 - crosses)
-            ret_out[g, ROW, a] = far.astype(BF16)
+            ret_out[g, ROW - 1, a] = far.astype(BF16)
             ret_y(a, g, ROW).start()
             acc[par, 0, a] = near
 
@@ -255,7 +255,7 @@
         par = lax.rem(g, 2)
         for a in (0, 1):
             ret_y(a, g, ROW).wait_recv()
-            total = acc[par, 0, a] + ret_in[g, ROW, a].astype(F32)
+            total = acc[par, 0, a] + ret_in[g, ROW - 1, a].astype(F32)
             dkv_stage[g, a] = total.T.astype(BF16)
             dkv_remote(a, g).start()
             dkv_local(a, g).start()
@@ -288,9 +288,10 @@
             tops[h // 2] = jnp.maximum(tops[h // 2], halves_max(sc))
 
     def dq_head(g, h):
-        left = jnp.concatenate([dsc[s, lanes(h, SHARD)] for s in range(SLOTS)], axis=1)
+        par = lax.rem(g, 2)
+        left = jnp.concatenate([dsc[par, s, lanes(h, SHARD)] for s in range(SLOTS)], axis=1)
         right = kv[0, g].reshape(SLOTS * SHARD, HEAD_SIZE)
-        dq_stage[g, :, lanes(h, HEAD_SIZE)] = (dot_nn(left, right) * inv_root).astype(BF16)
+        dq_stage[par, :, lanes(h, HEAD_SIZE)] = (dot_nn(left, right) * inv_root).astype(BF16)
 
     def exponentials(sbuf, hb, top, slots):
         total = jnp.zeros((SHARD, HEAD_SIZE), F32)
@@ -360,14 +361,15 @@
 
     def grads_step(g, s):
         values_t = kv[1, g, s].T
+        par = lax.rem(g, 2)
         far = lax.select(s > ROW, 1, 0)
         for h in range(width):
             g_h = qgo[1, g, :, head_cols(h)]
             p = sbufs[h % 2][s, h // 2] * twice(invs[far, h])
             dp = dot_nn(g_h, values_t)
             probs[head_rows(h)] = p.astype(BF16)
-            dsc[s, head_rows(h)] = (p * (dp - twice(deltas[h]))).astype(BF16)
-        dk = dot_nn(q_t[...], dsc[s]) * inv_root
+            dsc[par, s, head_rows(h)] = (p * (dp - twice(deltas[h]))).astype(BF16)
+        dk = dot_nn(q_t[...], dsc[par, s]) * inv_root
         dv = dot_nn(g_t[...], probs[...])
         return dk, dv
 
@@ -377,7 +379,6 @@
 
     def head_step(g, carry):
         par = lax.rem(g, 2)
-        before = jnp.maximum(g - 1, 0)
         wide_local(0, g).wait()
         wide_remote(0, g).wait_recv()
 
@@ -436,8 +437,7 @@
 
             lax.fori_loop(0, width // 2, far_softmax, 0)
 
-        @pl.when(g > 0)
-        def _():
+        def later_group(before):
             for d in (1, 3, 2):
                 kv_y(0, g, d).wait_recv()
             for a in (1, 2):
@@ -456,7 +456,15 @@
             tail = width // 2 - 1
             heads_step(g, (tail, 1), (tail, 0), before)
             heads_step(g, None, (tail, 1), None)
+
+        @pl.when((g > 0) & (g < n_kv - 1))
+        def _():
+            later_group(g - 1)
             send_dq(g - 1)
+
+        @pl.when(g == n_kv - 1)
+        def _():
+            later_group(None)
 
         def grads_of(i, carry_b):
             s = lax.select(i < 3, i + 5, lax.rem(i + 3, 5))
@@ -489,9 +497,9 @@
 
             @pl.when(i < 3)
             def _():
-                ret_out[g, s, 0] = dk.astype(BF16)
+                ret_out[g, s - 1, 0] = dk.astype(BF16)
                 ret_y(0, g, s).start()
-                ret_out[g, s, 1] = dv.astype(BF16)
+                ret_out[g, s - 1, 1] = dv.astype(BF16)
                 ret_y(1, g, s).start()
 
             @pl.when(i >= 3)
@@ -507,8 +515,8 @@
     lax.fori_loop(0, n_kv, head_step, 0)
     last = jnp.int32(n_kv - 1)
 
-    def last_dq(h, carry):
-        dq_head(last, h)
+    def last_dq(i, carry):
+        dq_head(last - 1 + i // width, lax.rem(i, width))
         return carry
 
     def drain_early(g, carry):
@@ -531,15 +539,19 @@
                 ret_x(a, g, d).wait_send()
             dkv_local(a, g).wait()
             dkv_remote(a, g).wait()
+        return carry
+
+    for g in range(n_kv - 2):
         dq_local(g).wait()
-        dq_remote(g).wait()
-        return carry
-
-    lax.fori_loop(0, width // 2, last_dq, 0)
+        dq_remote(g).wait_send()
+    half = width // 2
+    lax.fori_loop(0, half, last_dq, 0)
     back_y(last - 1)
     back_x(last, 2)
-    lax.fori_loop(width // 2, width, last_dq, 0)
+    lax.fori_loop(half, 3 * half, last_dq, 0)
     back_x(last, 3)
+    send_dq(last - 1)
+    lax.fori_loop(3 * half, 4 * half, last_dq, 0)
     send_dq(last)
     back_end(last - 1)
     lax.fori_loop(0, n_kv, drain_early, 0)
@@ -548,6 +560,11 @@
     back_end(last)
 
     drain(last, 0)
+    for g in range(n_kv):
+        if g >= n_kv - 2:
+            dq_local(g).wait()
+            dq_remote(g).wait_send()
+        dq_remote(g).wait_recv()
 
 
 def per_device(queries, key_matrix, value_matrix, attention_output, output_gradient, lengths):
@@ -583,11 +600,11 @@
             pltpu.VMEM((HEAD_SIZE, width * SHARD), BF16),
             pltpu.VMEM((HEAD_SIZE, width * SHARD), BF16),
             pltpu.VMEM((width * SHARD, SHARD), BF16),
-            pltpu.VMEM((SLOTS, width * SHARD, SHARD), BF16),
+            pltpu.VMEM((2, SLOTS, width * SHARD, SHARD), BF16),
             pltpu.VMEM((2, ROW + 1, 2, HEAD_SIZE, SHARD), F32),
-            pltpu.VMEM((n_kv, SLOTS, 2, HEAD_SIZE, SHARD), BF16),
-            pltpu.VMEM((n_kv, SLOTS, 2, HEAD_SIZE, SHARD), BF16),
-            pltpu.VMEM((n_kv, SHARD, wide), BF16),
+            pltpu.VMEM((n_kv, SLOTS - 1, 2, HEAD_SIZE, SHARD), BF16),
+            pltpu.VMEM((n_kv, SLOTS - 1, 2, HEAD_SIZE, SHARD), BF16),
+            pltpu.VMEM((2, SHARD, wide), BF16),
             pltpu.VMEM((n_kv, 2, SHARD, HEAD_SIZE), BF16),
             dma((3, n_kv)),
             dma((3, n_kv)),
@@ -607,7 +624,7 @@
             dma((2, n_kv)),
         ],
         compiler_params=pltpu.CompilerParams(
-            collective_id=0, has_side_effects=True, vmem_limit_bytes=62 * 1024 * 1024
+            collective_id=0, has_side_effects=True, vmem_limit_bytes=64 * 1024 * 1024 - 65536
         ),
         cost_estimate=pl.CostEstimate(
             flops=flops, bytes_accessed=10 * 1024 * 1024, transcendentals=flops // (10 * HEAD_SIZE)

time: 104 us -> 103 us (level)
  no operation moved by 1% of the time
where the time goes in v5:
time: 103 us
  Pallas kernels  102 us (99%)
    pallas_call x1, Pallas kernels, per_device(): pl.pallas_call(functools.partial(kernel, n_ctx, n_kv, width), out_shape=(...  99.8 us
    pallas_call x1, Pallas kernels, hand_over(): pl.pallas_call(functools.partial(hand_over_kernel, parts), out_shape=tupl...  2.6 us

profile of v5, /device:TPU:1, one launch (start us, length us, event | category | flops | bytes accessed | tf_op | source)
XLA Modules:
  0.0 103.1 jit_solution(8148581263028447050)
XLA Ops:
  0.6 99.8 %attention_backward.1 = (bf16[128,8192]{1,0:T(8,128)(2,1)}, bf16[128,1024]{1,0:T(8,128)(2,1)}, bf16[128,1024]{1,0:T(8,128)(2,1)}) custom-call(bf16[128,8192]{1,0:T(8,128)(2,1)} %q_in.1, bf16[128,1024]{1,0:T(8,128)(2,1)} %k_in.1, bf16[128,1024]{1,0:T(8,128)(2,1)} %v_in.1, bf16[128,8192]{1,0:T(8,128)(2,1)} %o_in.1, bf16[128,8192]{1,0:T(8,128)(2,1)} %g_in.1, ...), custom_call_target="tpu_custom_call" | custom-call | flops 21474836480 | bytes 10485760 | tf_op jit(solution)/shard_map/attention_backward/pallas_call | solution.py:580
  100.5 2.6 %hand_over.1 = (bf16[128,8192]{1,0:T(8,128)(2,1)}, bf16[128,1024]{1,0:T(8,128)(2,1)}, bf16[128,1024]{1,0:T(8,128)(2,1)}) custom-call(bf16[128,8192]{1,0:T(8,128)(2,1)} %get-tuple-element.6.dq_in, bf16[128,1024]{1,0:T(8,128)(2,1)} %get-tuple-element.7.dk_in, bf16[128,1024]{1,0:T(8,128)(2,1)} %get-tuple-element.8.dv_in), custom_call_target="tpu_custom_call" | custom-call | tf_op jit(solution)/shard_map/hand_over/pallas_call | solution.py:665

commit v6 on v5

--- a/solution.py
+++ b/solution.py
@@ -333,8 +333,7 @@
     def heads_step(g, new, old, before):
         if new is not None:
             h = 2 * new[0] + new[1]
-            if before is not None:
-                dq_head(before, h)
+            h_new = h
             q_new = qgo[0, g, :, lanes(h, HEAD_SIZE)]
             reach = None
         if old is not None:
@@ -351,6 +350,8 @@
                 sc = dot_nn(q_new, k_t[s]) * to_exp2 + bias[s]
                 sbufs[new[1]][s, new[0]] = sc
                 reach = halves_max(sc) if reach is None else jnp.maximum(reach, halves_max(sc))
+                if s == SLOTS - 1 and before is not None:
+                    dq_head(before, h_new)
         if new is not None:
             topss[new[1]][new[0]] = reach
         if old is not None:

time: 103 us -> 103 us (level)
  no operation moved by 1% of the time
where the time goes in v6:
time: 103 us
  Pallas kernels  102 us (99%)
    pallas_call x1, Pallas kernels, per_device(): pl.pallas_call(functools.partial(kernel, n_ctx, n_kv, width), out_shape=(...  99.7 us
    pallas_call x1, Pallas kernels, hand_over(): pl.pallas_call(functools.partial(hand_over_kernel, parts), out_shape=tupl...  2.6 us

profile of v6, /device:TPU:1, one launch (start us, length us, event | category | flops | bytes accessed | tf_op | source)
XLA Modules:
  0.0 102.9 jit_solution(15640018402493840888)
XLA Ops:
  0.6 99.7 %attention_backward.1 = (bf16[128,8192]{1,0:T(8,128)(2,1)}, bf16[128,1024]{1,0:T(8,128)(2,1)}, bf16[128,1024]{1,0:T(8,128)(2,1)}) custom-call(bf16[128,8192]{1,0:T(8,128)(2,1)} %q_in.1, bf16[128,1024]{1,0:T(8,128)(2,1)} %k_in.1, bf16[128,1024]{1,0:T(8,128)(2,1)} %v_in.1, bf16[128,8192]{1,0:T(8,128)(2,1)} %o_in.1, bf16[128,8192]{1,0:T(8,128)(2,1)} %g_in.1, ...), custom_call_target="tpu_custom_call" | custom-call | flops 21474836480 | bytes 10485760 | tf_op jit(solution)/shard_map/attention_backward/pallas_call | solution.py:581
  100.3 2.6 %hand_over.1 = (bf16[128,8192]{1,0:T(8,128)(2,1)}, bf16[128,1024]{1,0:T(8,128)(2,1)}, bf16[128,1024]{1,0:T(8,128)(2,1)}) custom-call(bf16[128,8192]{1,0:T(8,128)(2,1)} %get-tuple-element.6.dq_in, bf16[128,1024]{1,0:T(8,128)(2,1)} %get-tuple-element.7.dk_in, bf16[128,1024]{1,0:T(8,128)(2,1)} %get-tuple-element.8.dv_in), custom_call_target="tpu_custom_call" | custom-call | tf_op jit(solution)/shard_map/hand_over/pallas_call | solution.py:666
